TPU v7x, 256 devices: a whole 4x4x8 slice. The times are simulated.
256 devices in a mesh: stn: 32 (over y, z_hi, core), tm: 8 (over z_lo, x).
Axes of the slice: x: 4, y: 4, z: 8 (z_hi: 4, z_lo: 2; z = z_hi * 2 + z_lo), core: 2. Of those that a mesh axis runs over, the one named last changes fastest.
Arguments:
- voltages: int32 [512, 2, 131072], P('stn', None, 'tm'), may hold values from -127 to 127
- filter_taps: float32 [16, 1024], replicated, may hold values from -1.5 to 1.5
- reference_channel: int32 [1], replicated, may hold values from 0 to 511
- basis_inputs: int32 [8], replicated, may hold values from 0 to 511, as said below
Outputs:
- covariance: bfloat16 [512, 512, 1024], P(('stn', 'tm'))
- projection: float32 [512, 128], P(('stn', 'tm'))
- subspace_power: float32 [512, 128], P('stn', 'tm')
Inputs may be any that keep to these rules, and one draw needn't show every extreme that they name: `basis_inputs`: 8 distinct input indices.
All inputs are finite; a program needn't handle non-finite values.
Results may differ from a plain program's by a relative error of at most 0.012.
Values may be sent and summed in bfloat16 or wider, within the bound.
A program may use at most 64 MiB of HBM per device.

v0:
```python
import math

import jax
import jax.numpy as jnp
from jax import lax
from jax.sharding import PartitionSpec as P

NFFT = 1024
FCH = 512


def passed_along(block, axis, distance):
    devices = range(lax.axis_size(axis))
    route = [(i - distance, i) for i in devices if i - distance in devices]
    return lax.ppermute(block, axis, route)


def in_one_piece(arrays, axis, split_dim, concat_dim, along):
    ends, at = ([], 0)
    for a in arrays[:-1]:
        at += a.shape[along]
        ends.append(at)
    both = jnp.concatenate(arrays, axis=along)
    return tuple(
        jnp.split(
            lax.all_to_all(both, axis, split_axis=split_dim, concat_axis=concat_dim, tiled=True),
            ends,
            axis=along,
        )
    )


def spread(shard, axis, root):
    mine = lax.axis_index(axis) == root
    return lax.psum(jnp.where(mine, shard, jnp.zeros_like(shard)), axis)


def transform_tables():
    sample = jnp.arange(NFFT, dtype=jnp.int32)
    channel = jnp.arange(FCH, dtype=jnp.int32)
    phase = sample[:, None] * channel[None, :] % NFFT
    angle = phase.astype(jnp.float32) * (2.0 * math.pi / NFFT)
    factor = 1.0 / math.sqrt(NFFT)
    cosine = jnp.cos(angle) * factor
    sine = jnp.sin(angle) * factor
    table_re = jnp.stack([cosine, -sine], axis=2).reshape(NFFT, 2 * FCH).astype(jnp.bfloat16)
    table_im = jnp.stack([sine, cosine], axis=2).reshape(NFFT, 2 * FCH).astype(jnp.bfloat16)
    return (table_re, table_im)


def orthonormal(col_real, col_imag):
    basis_real = []
    basis_imag = []
    for column in range(col_real.shape[1]):
        vec_real = col_real[:, column]
        vec_imag = col_imag[:, column]
        for former in range(column):
            q_real = basis_real[former]
            q_imag = basis_imag[former]
            inner_real = jnp.sum(q_real * vec_real + q_imag * vec_imag)
            inner_imag = jnp.sum(q_real * vec_imag - q_imag * vec_real)
            vec_real = vec_real - (q_real * inner_real - q_imag * inner_imag)
            vec_imag = vec_imag - (q_real * inner_imag + q_imag * inner_real)
        inverse = lax.rsqrt(jnp.sum(vec_real * vec_real + vec_imag * vec_imag) + 1e-06)
        basis_real.append(vec_real * inverse)
        basis_imag.append(vec_imag * inverse)
    return (jnp.stack(basis_real, axis=1), jnp.stack(basis_imag, axis=1))


def block_sums(part_real, part_imag):
    sum_real = jnp.einsum("itc,jtc->cij", part_real, part_real, preferred_element_type=jnp.float32)
    sum_real = sum_real + jnp.einsum(
        "itc,jtc->cij", part_imag, part_imag, preferred_element_type=jnp.float32
    )
    sum_imag = jnp.einsum("itc,jtc->cij", part_imag, part_real, preferred_element_type=jnp.float32)
    sum_imag = sum_imag - jnp.einsum(
        "itc,jtc->cij", part_real, part_imag, preferred_element_type=jnp.float32
    )
    return (sum_real, sum_imag)


def blockwise_covariance(full_real, full_imag, blocks, frames):
    inputs_all = full_real.shape[0]
    chans = full_real.shape[2]

    def add_block(index, total):
        first = index * frames
        part_real = lax.dynamic_slice_in_dim(full_real, first, frames, 1)
        part_imag = lax.dynamic_slice_in_dim(full_imag, first, frames, 1)
        sum_real, sum_imag = block_sums(part_real, part_imag)
        terms = jnp.concatenate([sum_real, sum_imag], axis=2)
        rounded = lax.optimization_barrier(terms.astype(jnp.bfloat16)).astype(jnp.float32)
        return total + rounded

    start = jnp.zeros((chans, inputs_all, 2 * inputs_all), jnp.float32)
    return lax.fori_loop(0, blocks, add_block, start)


def on_device(voltages, filter_taps, reference_channel, basis_inputs):
    blocks = lax.axis_size("tm")
    local_inputs = voltages.shape[0]
    inputs_all = local_inputs * lax.axis_size("stn")
    frames = voltages.shape[2] // NFFT
    spectra_total = frames * blocks
    tap_count = filter_taps.shape[0]
    signal = (
        (voltages.astype(jnp.float32) / 64.0)
        .astype(jnp.bfloat16)
        .reshape(local_inputs, 2, frames, NFFT)
    )
    earlier = passed_along(signal[:, :, frames - (tap_count - 1) :, :], "tm", 1)
    extended = jnp.concatenate([earlier, signal], axis=2)
    accum = jnp.zeros((local_inputs, 2, frames, NFFT), jnp.float32)
    for tap_index in range(tap_count):
        accum = accum + filter_taps[tap_index] * extended[
            :, :, tap_index : tap_index + frames, :
        ].astype(jnp.float32)
    filtered = accum.astype(jnp.bfloat16)
    table_re, table_im = transform_tables()
    spectra = jnp.einsum(
        "itn,nc->itc", filtered[:, 0], table_re, preferred_element_type=jnp.float32
    )
    spectra = spectra + jnp.einsum(
        "itn,nc->itc", filtered[:, 1], table_im, preferred_element_type=jnp.float32
    )
    spectra = spectra.astype(jnp.bfloat16)
    rows_iota = jnp.arange(inputs_all, dtype=jnp.int32)[:, None]
    turned = lax.all_to_all(spectra, "stn", split_axis=2, concat_axis=0, tiled=True)
    chan_count = turned.shape[2] // 2
    chan_owned = chan_count // blocks
    split = turned.reshape(inputs_all, frames, chan_count, 2)
    chan_real = split[:, :, :, 0]
    chan_imag = split[:, :, :, 1]
    moved_real, moved_imag = in_one_piece((chan_real, chan_imag), "tm", 2, 1, 0)
    summed = blockwise_covariance(moved_real, moved_imag, blocks, frames)
    averaged = summed / spectra_total
    covariance = averaged.astype(jnp.bfloat16)
    highest = lax.Precision.HIGHEST
    selector = rows_iota == basis_inputs[None, :]
    ref_index = reference_channel[0]
    root_index = ref_index // chan_owned
    local_index = ref_index % chan_owned
    ref_rows = lax.dynamic_slice_in_dim(averaged, local_index, 1, 0)[0]
    onehot = selector.astype(jnp.float32)
    picked = jnp.stack(
        [
            jnp.dot(ref_rows[:, :inputs_all], onehot, precision=highest),
            jnp.dot(ref_rows[:, inputs_all:], onehot, precision=highest),
        ]
    )
    picked = spread(picked.astype(jnp.bfloat16), ("stn", "tm"), root_index).astype(picked.dtype)
    col_real = picked[0]
    col_imag = picked[1]
    basis_real, basis_imag = orthonormal(col_real, col_imag)
    cov_real = averaged[:, :, :inputs_all]
    cov_imag = averaged[:, :, inputs_all:]
    prod_real = jnp.einsum("cij,jk->cik", cov_real, basis_real, precision=highest)
    prod_real = prod_real - jnp.einsum("cij,jk->cik", cov_imag, basis_imag, precision=highest)
    prod_imag = jnp.einsum("cij,jk->cik", cov_real, basis_imag, precision=highest)
    prod_imag = prod_imag + jnp.einsum("cij,jk->cik", cov_imag, basis_real, precision=highest)
    proj_real = jnp.einsum("ik,cil->ckl", basis_real, prod_real, precision=highest)
    proj_real = proj_real + jnp.einsum("ik,cil->ckl", basis_imag, prod_imag, precision=highest)
    proj_imag = jnp.einsum("ik,cil->ckl", basis_real, prod_imag, precision=highest)
    proj_imag = proj_imag - jnp.einsum("ik,cil->ckl", basis_imag, prod_real, precision=highest)
    projection = jnp.concatenate(
        [proj_real.reshape(chan_owned, -1), proj_imag.reshape(chan_owned, -1)], axis=1
    )
    low_real = basis_real.astype(jnp.bfloat16)
    low_imag = basis_imag.astype(jnp.bfloat16)
    sub_real = jnp.einsum("ik,itc->kct", low_real, chan_real, preferred_element_type=jnp.float32)
    sub_real = sub_real + jnp.einsum(
        "ik,itc->kct", low_imag, chan_imag, preferred_element_type=jnp.float32
    )
    sub_imag = jnp.einsum("ik,itc->kct", low_real, chan_imag, preferred_element_type=jnp.float32)
    sub_imag = sub_imag - jnp.einsum(
        "ik,itc->kct", low_imag, chan_real, preferred_element_type=jnp.float32
    )
    subspace_power = jnp.sum(sub_real * sub_real + sub_imag * sub_imag, axis=0)
    return (covariance, projection, subspace_power)


def solution(mesh):
    return jax.shard_map(
        on_device,
        mesh=mesh,
        in_specs=(P("stn", None, "tm"), P(), P(), P()),
        out_specs=(P(("stn", "tm"), None, None), P(("stn", "tm"), None), P("stn", "tm")),
        check_vma=False,
    )
```

profile of v0, /device:TPU:1, one launch (start us, length us, event | category | flops | bytes accessed | tf_op | source)
XLA Modules:
  0.0 384.4 jit_solution(3976000527259442747)
XLA Ops:
  6.2 4.9 %collective-permute-start = (bf16[16,2,15,1024]{3,0,2,1:T(8,128)(2,1)}, bf16[16,2,15,1024]{3,0,2,1:T(8,128)(2,1)}, u32[]{:S(2)}, u32[]{:S(2)}) collective-permute-start(bf16[16,2,15,1024]{3,0,2,1:T(8,128)(2,1)} %copy.41), channel_id=1, source_target_pairs={{0,1},{1,2},{2,3},{3,4},{4,5},{5,6},{6,7},{8,9},{9,10},{10,11},{11... | collective-permute-start | bytes 2949128 | tf_op jit(solution)/shard_map/ppermute | solution.py:15
  11.1 8.0 %fusion.30 = bf16[1024,512,1]{1,0,2:T(8,128)(2,1)S(1)} fusion(), kind=kLoop, calls=%fused_computation.74 | loop fusion | flops 8388608 | bytes 1048576 | tf_op jit(solution)/shard_map/convert.6
  19.1 8.6 %negate_convert_fusion = (bf16[1024,512,1]{1,0,2:T(8,128)(2,1)S(1)}, bf16[1024,512,1]{1,0,2:T(8,128)(2,1)S(1)}) fusion(), kind=kLoop, calls=%fused_computation.58 | loop fusion | flops 9961472 | bytes 2097152 | tf_op jit(solution)/shard_map/convert.9
  29.4 6.3 %copy.45 = bf16[1024,512,2]{0,2,1:T(2,128)(2,1)} copy(bf16[1024,512,2]{1,0,2:T(8,128)(2,1)} %get-tuple-element.294) | data formatting | bytes 4194304 | tf_op jit(solution)/shard_map/stack | solution.py:47
  35.7 4.1 %convert_element_type.151 = bf16[1024,1024]{0,1:T(8,128)(2,1)} reshape(bf16[1024,512,2]{0,2,1:T(2,128)(2,1)} %copy.45) | data formatting | bytes 4194304 | tf_op jit(solution)/shard_map/convert_element_type | solution.py:47
  39.8 4.1 %copy.43 = bf16[1024,512,2]{0,2,1:T(2,128)(2,1)} copy(bf16[1024,512,2]{1,0,2:T(8,128)(2,1)S(1)} %get-tuple-element.293) | data formatting | bytes 4194304 | tf_op jit(solution)/shard_map/stack | solution.py:46
  48.5 6.2 %add_convert_fusion.1 = bf16[16,2,16,1024]{3,2,0,1:T(8,128)(2,1)S(1)} fusion(bf16[16,2,16,1024]{3,2,0,1:T(8,128)(2,1)S(1)} %copy.60, bf16[16,2,15,1024]{3,2,0,1:T(8,128)(2,1)S(1)} %copy.42, f32[1024]{0:T(1024)S(1)} %bitcast.183, f32[1024]{0:T(1024)S(1)} %bitcast.184, f32[1024]{0:T(1024)S(1)} %bitcast.170, f32[1024]{0:T(1024)S(1)} %bitcast.171, ...), kind=kLoop, calls=%fused_computation.63 | loop fusion | flops 48758784 | bytes 3145728 | tf_op jit(solution)/shard_map/convert_element_type | solution.py:118
  56.2 4.7 %copy.47 = bf16[16,16,1024]{1,0,2:T(8,128)(2,1)} copy(bf16[16,16,1024]{2,1,0:T(8,128)(2,1)S(1)} %fusion.34) | data formatting | bytes 1048576 | tf_op jit(solution)/shard_map/convert_element_type | solution.py:126
  60.9 6.4 %reshape.156 = bf16[32,2,4096]{2,1,0:T(2,128)(2,1)S(1)} reshape(bf16[1024,16,16]{2,1,0:T(8,128)(2,1)} %bitcast.127) | data formatting | bytes 1048576
  67.3 30.0 %all_to_all.30 = bf16[32,2,4096]{2,1,0:T(2,128)(2,1)S(1)} all-to-all(bf16[32,2,4096]{2,1,0:T(2,128)(2,1)S(1)} %reshape.156), channel_id=1, replica_groups=mesh['stn'=32,'tm'=8] {'stn'}, dimensions={0} | all-to-all | bytes 1048576 | tf_op jit(solution)/shard_map/all_to_all | solution.py:128
  97.3 4.1 %reshape.157 = bf16[1024,16,16]{2,1,0:T(8,128)(2,1)} reshape(bf16[32,2,4096]{2,1,0:T(2,128)(2,1)S(1)} %all_to_all.30) | data formatting | bytes 1048576
  101.5 7.1 %copy.48 = bf16[16,16,32,32]{0,2,1,3:T(8,128)(2,1)} copy(bf16[16,16,32,32]{1,0,3,2:T(8,128)(2,1)} %bitcast.128) | data formatting | bytes 1048576 | tf_op jit(solution)/shard_map/all_to_all | solution.py:128
  108.5 7.8 %reshape.146 = bf16[512,16,16,2]{0,1,3,2:T(8,128)(2,1)S(1)} reshape(bf16[32,16,16,32]{1,0,2,3:T(8,128)(2,1)} %bitcast.129) | data formatting | bytes 1048576 | tf_op jit(solution)/shard_map/reshape | solution.py:131
  117.8 4.5 %all-to-all-start.1 = ((bf16[1024,16,16]{0,1,2:T(8,128)(2,1)}), bf16[1024,16,16]{0,1,2:T(8,128)(2,1)S(1)}, u32[]{:S(2)}, u32[]{:S(2)}) async-start(bf16[1024,16,16]{0,1,2:T(8,128)(2,1)} %copy.51), calls=%async_computation.1 | async-start | bytes 1048576 | tf_op jit(solution)/shard_map/all_to_all | solution.py:26
  123.0 8.3 %all-to-all-done.1 = bf16[1024,16,16]{0,1,2:T(8,128)(2,1)S(1)} async-done(((bf16[1024,16,16]{0,1,2:T(8,128)(2,1)}), bf16[1024,16,16]{0,1,2:T(8,128)(2,1)S(1)}, u32[]{:S(2)}, u32[]{:S(2)}) %all-to-all-start.1) | async-done | bytes 524320 | tf_op jit(solution)/shard_map/all_to_all | solution.py:26
  131.4 53.6 %while.14 = (s32[]{:T(128)}, f32[2,512,1024]{1,2,0:T(8,128)}, bf16[512,128,2]{0,1,2:T(8,128)(2,1)S(1)}, bf16[512,128,2]{0,1,2:T(8,128)(2,1)S(1)}, s32[]{:T(128)}, /*index=5*/s32[]{:T(128)}, s32[]{:T(128)}, s32[]{:T(128)}) while((s32[]{:T(128)}, f32[2,512,1024]{1,2,0:T(8,128)}, bf16[512,128,2]{0,1,2:T(8,128)(2,1)S(1)}, ...), condition=%wide.region_1.2_spmd.clone, body=%wide.region_0.1_spmd.clone.sunk | while | flops 76546048 | bytes 25364628 | solution.py:96
  138.3 4.9 %select_add_fusion.2 = f32[2,512,1024]{1,2,0:T(8,128)} fusion(f32[2,512,1024]{1,2,0:T(8,128)} %get-tuple-element.369, bf16[2,512,1024]{1,2,0:T(8,128)(2,1)S(1)} %pad_maximum_fusion.7, pred[]{:T(512)S(6)} %compare.19), kind=kLoop, calls=%fused_computation.clone.1 | loop fusion | flops 3145728 | bytes 10485761 | tf_op jit(solution)/shard_map/while/body/eval_jaxpr/add | solution.py:93
  145.3 4.9 %select_add_fusion.2 = f32[2,512,1024]{1,2,0:T(8,128)} fusion(f32[2,512,1024]{1,2,0:T(8,128)} %get-tuple-element.369, bf16[2,512,1024]{1,2,0:T(8,128)(2,1)S(1)} %pad_maximum_fusion.7, pred[]{:T(512)S(6)} %compare.19), kind=kLoop, calls=%fused_computation.clone.1 | loop fusion | flops 3145728 | bytes 10485761 | tf_op jit(solution)/shard_map/while/body/eval_jaxpr/add | solution.py:93
  152.3 4.9 %select_add_fusion.2 = f32[2,512,1024]{1,2,0:T(8,128)} fusion(f32[2,512,1024]{1,2,0:T(8,128)} %get-tuple-element.369, bf16[2,512,1024]{1,2,0:T(8,128)(2,1)S(1)} %pad_maximum_fusion.7, pred[]{:T(512)S(6)} %compare.19), kind=kLoop, calls=%fused_computation.clone.1 | loop fusion | flops 3145728 | bytes 10485761 | tf_op jit(solution)/shard_map/while/body/eval_jaxpr/add | solution.py:93
  159.2 4.9 %select_add_fusion.2 = f32[2,512,1024]{1,2,0:T(8,128)} fusion(f32[2,512,1024]{1,2,0:T(8,128)} %get-tuple-element.369, bf16[2,512,1024]{1,2,0:T(8,128)(2,1)S(1)} %pad_maximum_fusion.7, pred[]{:T(512)S(6)} %compare.19), kind=kLoop, calls=%fused_computation.clone.1 | loop fusion | flops 3145728 | bytes 10485761 | tf_op jit(solution)/shard_map/while/body/eval_jaxpr/add | solution.py:93
  166.2 4.9 %select_add_fusion.2 = f32[2,512,1024]{1,2,0:T(8,128)} fusion(f32[2,512,1024]{1,2,0:T(8,128)} %get-tuple-element.369, bf16[2,512,1024]{1,2,0:T(8,128)(2,1)S(1)} %pad_maximum_fusion.7, pred[]{:T(512)S(6)} %compare.19), kind=kLoop, calls=%fused_computation.clone.1 | loop fusion | flops 3145728 | bytes 10485761 | tf_op jit(solution)/shard_map/while/body/eval_jaxpr/add | solution.py:93
  173.2 4.9 %select_add_fusion.2 = f32[2,512,1024]{1,2,0:T(8,128)} fusion(f32[2,512,1024]{1,2,0:T(8,128)} %get-tuple-element.369, bf16[2,512,1024]{1,2,0:T(8,128)(2,1)S(1)} %pad_maximum_fusion.7, pred[]{:T(512)S(6)} %compare.19), kind=kLoop, calls=%fused_computation.clone.1 | loop fusion | flops 3145728 | bytes 10485761 | tf_op jit(solution)/shard_map/while/body/eval_jaxpr/add | solution.py:93
  180.2 4.9 %select_add_fusion.2 = f32[2,512,1024]{1,2,0:T(8,128)} fusion(f32[2,512,1024]{1,2,0:T(8,128)} %get-tuple-element.369, bf16[2,512,1024]{1,2,0:T(8,128)(2,1)S(1)} %pad_maximum_fusion.7, pred[]{:T(512)S(6)} %compare.19), kind=kLoop, calls=%fused_computation.clone.1 | loop fusion | flops 3145728 | bytes 10485761 | tf_op jit(solution)/shard_map/while/body/eval_jaxpr/add | solution.py:93
  185.0 5.4 %copy.54 = f32[2,512,1024]{2,1,0:T(8,128)} copy(f32[2,512,1024]{1,2,0:T(8,128)} %get-tuple-element.82) | data formatting | bytes 8388608 | tf_op jit(solution)/shard_map/while | solution.py:96
  190.4 4.2 %broadcast_multiply_fusion = (f32[2,512,1024]{2,1,0:T(8,128)S(1)}, bf16[2,512,1024]{2,1,0:T(8,128)(2,1)}) fusion(f32[2,512,1024]{2,1,0:T(8,128)} %copy.54), kind=kLoop, calls=%fused_computation.57 | loop fusion | flops 2097152 | bytes 10485760 | tf_op jit(solution)/shard_map/div | solution.py:136
  197.8 74.6 %psum.7 = bf16[2,512,8]{1,2,0:T(8,128)(2,1)S(1)} all-reduce(bf16[2,512,8]{1,2,0:T(8,128)(2,1)S(1)} %maximum_select_fusion), channel_id=1, replica_groups=mesh['stn'=32,'tm'=8] {'stn','tm'}, use_global_device_ids=true, to_apply=%region_2.3 | all-reduce | flops 8192 | bytes 32768 | tf_op jit(solution)/shard_map/psum | solution.py:35
  277.0 8.2 %add_reduce_fusion.6 = (f32[]{:T(128)}, f32[]{:T(128)}, f32[]{:T(128)}, f32[]{:T(128)}, f32[]{:T(128)}, /*index=5*/f32[]{:T(128)}, f32[]{:T(128)}, f32[]{:T(128)...) fusion(f32[512]{0:T(512)S(1)} %bitcast.164, ...), kind=kLoop, calls=%fused_computation.166 | loop fusion | flops 50164 | bytes 61540 | tf_op jit(solution)/shard_map/reduce_sum | solution.py:60
  287.8 7.0 %add_reduce_fusion.5 = (f32[]{:T(128)}, f32[]{:T(128)}, f32[]{:T(128)}, f32[]{:T(128)}, f32[]{:T(128)}, /*index=5*/f32[]{:T(128)}, f32[]{:T(128)}, f32[]{:T(128)...) fusion(f32[512]{0:T(512)S(1)} %get-tuple-element.276, ...), kind=kLoop, calls=%fused_computation.162 | loop fusion | flops 41974 | bytes 53332 | tf_op jit(solution)/shard_map/reduce_sum | solution.py:60
  297.3 5.6 %add_reduce_fusion.4 = (f32[]{:T(128)}, f32[]{:T(128)}, f32[]{:T(128)}, f32[]{:T(128)}, f32[]{:T(128)}, /*index=5*/f32[]{:T(128)}, f32[]{:T(128)}, f32[]{:T(128)...) fusion(f32[512]{0:T(512)S(1)} %get-tuple-element.261, ...), kind=kLoop, calls=%fused_computation.158 | loop fusion | flops 33784 | bytes 45124 | tf_op jit(solution)/shard_map/reduce_sum | solution.py:60
  305.5 4.6 %add_reduce_fusion.3 = (f32[]{:T(128)}, f32[]{:T(128)}, f32[]{:T(128)}, f32[]{:T(128)}, f32[]{:T(128)}, /*index=5*/f32[]{:T(128)}, f32[512]{0:T(512)S(1)}, f32[5...) fusion(f32[512]{0:T(512)S(1)} %get-tuple-element.248, ...), kind=kLoop, calls=%fused_computation.154 | loop fusion | flops 25594 | bytes 36916 | tf_op jit(solution)/shard_map/reduce_sum | solution.py:60
  322.6 35.1 %subtract_multiply_fusion = (f32[512,1]{0,1:T(1,128)S(1)}, f32[512,1]{0,1:T(1,128)S(1)}, f32[512,1]{0,1:T(1,128)S(1)}, f32[512,1]{0,1:T(1,128)S(1)}, f32[512,1]{...) fusion(f32[512,1]{0,1:T(1,128)S(1)} %get-tuple-element.318, ...), kind=kLoop, calls=%fused_computation.141 | loop fusion | flops 107008 | bytes 57596 | tf_op jit(solution)/shard_map/mul | solution.py:66
  357.6 8.8 %subtract_multiply_fusion.1 = f32[512,1]{0,1:T(1,128)S(1)} fusion(f32[512,1]{0,1:T(1,128)S(1)} %get-tuple-element.211, f32[512,1]{0,1:T(1,128)S(1)} %get-tuple-element.212, f32[512,1]{0,1:T(1,128)S(1)} %get-tuple-element.213, f32[512,1]{0,1:T(1,128)S(1)} %get-tuple-element.214, f32[512,1]{0,1:T(1,128)S(1)} %get-tuple-element.215, ...), kind=kLoop, calls=%fused_computation.143 | loop fusion | flops 14848 | bytes 32828 | tf_op jit(solution)/shard_map/mul | solution.py:65
  (109 shorter events, 74.6 us)
Async XLA Ops:
  6.2 40.5 %collective-permute-start = (bf16[16,2,15,1024]{3,0,2,1:T(8,128)(2,1)}, bf16[16,2,15,1024]{3,0,2,1:T(8,128)(2,1)}, u32[]{:S(2)}, u32[]{:S(2)}) collective-permute-start(bf16[16,2,15,1024]{3,0,2,1:T(8,128)(2,1)} %copy.41), channel_id=1, source_target_pairs={{0,1},{1,2},{2,3},{3,4},{4,5},{5,6},{6,7},{8,9},{9,10},{10,11},{11... | collective-permute-start | bytes 2949128 | tf_op jit(solution)/shard_map/ppermute | solution.py:15
  43.8 2.8 copy-start.2
  48.4 6.2 %copy-start.1 = (bf16[1024,1024]{0,1:T(8,128)(2,1)S(1)}, bf16[1024,1024]{0,1:T(8,128)(2,1)}, u32[]{:S(2)}) copy-start(bf16[1024,1024]{0,1:T(8,128)(2,1)} %convert_element_type.151) | copy-start | bytes 6291460
  117.8 13.5 %all-to-all-start.1 = ((bf16[1024,16,16]{0,1,2:T(8,128)(2,1)}), bf16[1024,16,16]{0,1,2:T(8,128)(2,1)S(1)}, u32[]{:S(2)}, u32[]{:S(2)}) async-start(bf16[1024,16,16]{0,1,2:T(8,128)(2,1)} %copy.51), calls=%async_computation.1 | async-start | bytes 1048576 | tf_op jit(solution)/shard_map/all_to_all | solution.py:26
  194.6 1.9 copy-start
  194.6 1.9 copy-start.3
where the time goes:
time: 387 us; the launch traced here: 384 us
  other arithmetic  159 us (41%)
  blocking collectives  105 us (27%)
  local copies, waits for them, and re-layouts  61.9 us (16%)
  matrix products  34.3 us (9%)
  starting transfers between devices  9.4 us (2%)
  waiting for transfers between devices  8.28 us (2%)
  between operations  6.91 us (2%)
    psum x1, blocking collectives, spread(): return lax.psum(jnp.where(mine, shard, jnp.zeros_like(shard)), axis)  74.6 us
    add x8, other arithmetic, add_block(): return total + rounded  36.8 us
    mul x1, other arithmetic, orthonormal(): basis_imag.append(vec_imag * inverse)  35.1 us
    reduce_sum x7, other arithmetic, orthonormal(): inner_real = jnp.sum(q_real * vec_real + q_imag * vec_imag)  31.3 us
    all_to_all x1, blocking collectives, on_device(): lax.all_to_all(spectra, 'stn', split_axis=2, concat_axis=0, tiled=True)  30 us
    another operation x2, other arithmetic  16.6 us
    reduce_sum x8, other arithmetic, orthonormal(): jnp.sum(vec_real * vec_real + vec_imag * vec_imag) + 1e-06  13.6 us
    unnamed x13, local copies, waits for them, and re-layouts  13.3 us
  transfers between devices with their start and end apart: 2, of which 1 were waited for; matrix products, arithmetic and copies ran while one was open for 9% of the time, Pallas kernels for 0%

commit v1 on v0

v1 whole, which is shorter than its diff:
```python
import functools
import math

import jax
import jax.numpy as jnp
import numpy as np
from jax import lax
from jax.experimental import pallas as pl
from jax.experimental.pallas import tpu as pltpu
from jax.sharding import PartitionSpec as P

NFFT = 1024
FCH = 512
TAPS = 16
K = 8
INPUTS = 512
SPECTRA = 128
STN = 32
TM = 8
LOCAL = INPUTS // STN
FRAMES = SPECTRA // TM
SUB = NFFT // 128
Q = 2 * SUB
SPILL = TAPS - 1
TILES = 4
CH = 1
NCH = TILES // CH
WIDE = CH * 128
MESH = pl.DeviceIdType.MESH
F32 = jnp.float32
BF16 = jnp.bfloat16
HIGHEST = lax.Precision.HIGHEST


def transform_table():
    phase = np.arange(NFFT)[:, None] * np.arange(FCH)[None, :] % NFFT
    angle = phase.astype(np.float32) * np.float32(2.0 * math.pi / NFFT)
    factor = np.float32(1.0 / math.sqrt(NFFT))
    cosine, sine = np.cos(angle) * factor, np.sin(angle) * factor
    table_re = np.stack([cosine, -sine], axis=2)
    table_im = np.stack([sine, cosine], axis=2)
    both = np.stack([table_re.reshape(SUB, 128, FCH, 2), table_im.reshape(SUB, 128, FCH, 2)], axis=1)
    both = both.reshape(2 * NFFT, 2, 16, TILES, 2, 2, 2)
    both = both.transpose(3, 0, 1, 4, 2, 5, 6)
    both = both.reshape(NCH, CH, 2 * NFFT, 256).transpose(0, 2, 1, 3)
    return both.reshape(NCH, 2 * NFFT, 2 * WIDE).astype(jnp.bfloat16)


def butterfly(blocks, lane):
    blocks = list(blocks)
    for bit in range(4):
        step, shift = 1 << bit, 4 << bit
        low = (lane & shift) == 0
        for a in range(16):
            if a & step:
                continue
            first, second = blocks[a], blocks[a | step]
            blocks[a] = jnp.where(low, first, pltpu.roll(second, shift, 1))
            blocks[a | step] = jnp.where(low, pltpu.roll(first, 128 - shift, 1), second)
    return blocks


def gram_schmidt(vec_re, vec_im):
    row = lax.broadcasted_iota(jnp.int32, (K, 1), 0)
    for k in range(K):
        w_re, w_im = vec_re[k : k + 1], vec_im[k : k + 1]
        in_re = jnp.sum(w_re * vec_re + w_im * vec_im, axis=1, keepdims=True)
        in_im = jnp.sum(w_re * vec_im - w_im * vec_re, axis=1, keepdims=True)
        inverse = lax.rsqrt(in_re[k : k + 1] + 1e-06)
        q_re, q_im = w_re * inverse, w_im * inverse
        c_re = jnp.where(row > k, in_re * inverse, 0.0)
        c_im = jnp.where(row > k, in_im * inverse, 0.0)
        new_re = vec_re - (q_re * c_re - q_im * c_im)
        new_im = vec_im - (q_re * c_im + q_im * c_re)
        vec_re = jnp.where(row == k, q_re, new_re)
        vec_im = jnp.where(row == k, q_im, new_im)
    return vec_re, vec_im


def channelise_kernel(
    volt, taps, table_hbm, ref_chan, basis_in,
    u, v, basis,
    table, tap_rows, frames_f, lhs, halo_out, halo_in, send1, send2, cols_out, cols_a, cols_b, cols_c,
    table_sem, halo_ss, halo_rs, ss1, rs1, ss2, rs2, css, crs_a, crs_b, crs_c,
):
    s = lax.axis_index("stn")
    t = lax.axis_index("tm")
    barrier = pltpu.get_barrier_semaphore()

    @pl.loop(1, STN)
    def _(d):
        pl.semaphore_signal(barrier, 1, device_id={"stn": lax.rem(s + d, STN)}, device_id_type=MESH)

    @pl.loop(1, TM)
    def _(d):
        pl.semaphore_signal(barrier, 1, device_id={"tm": lax.rem(t + d, TM)}, device_id_type=MESH)

    load_table = pltpu.make_async_copy(table_hbm, table, table_sem)
    load_table.start()

    for sub in range(SUB):
        part = taps[:, sub * 128 : (sub + 1) * 128] * (1.0 / 64.0)
        for p in range(2):
            tap_rows[pl.ds(sub * 2 + p, TAPS, stride=Q), :] = part

    def filter_frames(spill):
        @pl.loop(0, LOCAL * 2)
        def _(step):
            i, half = step // 2, lax.rem(step, 2)
            base = pl.multiple_of(i * (FRAMES * Q) + half * 8, 8)
            x = [volt[pl.ds(base + f * Q, 8), :].astype(F32) for f in range(FRAMES)]
            tap = [tap_rows[pl.ds(pl.multiple_of(k * Q + half * 8, 8), 8), :] for k in range(TAPS)]
            for f in range(SPILL if spill else FRAMES):
                acc = None
                for j in range(f + 1, FRAMES) if spill else range(f + 1):
                    k = j - f - 1 if spill else SPILL - f + j
                    term = tap[k] * x[j]
                    acc = term if acc is None else acc + term
                row = pl.multiple_of((f * LOCAL + i) * Q + half * 8, 8)
                frames_f[pl.ds(row, 8), :] = acc

        rows = (SPILL if spill else FRAMES) * LOCAL
        for q in range(Q):
            lhs[0:rows, q * 128 : (q + 1) * 128] = frames_f[pl.ds(q, rows, stride=Q), :].astype(BF16)

    def chunk_of(block, step):
        return lax.rem(block // (2 * CH) + 1 + step, NCH)

    def halo_copy(j):
        return pltpu.make_async_remote_copy(
            src_ref=halo_out.at[j],
            dst_ref=halo_in.at[j],
            send_sem=halo_ss.at[j],
            recv_sem=halo_rs.at[j],
            device_id={"tm": lax.rem(t + 1, TM)},
            device_id_type=MESH,
        )

    def stage1_copy(j, to):
        return pltpu.make_async_remote_copy(
            src_ref=send1.at[j, pl.ds(pl.multiple_of(to * LOCAL, LOCAL), LOCAL)],
            dst_ref=u.at[j, pl.ds(pl.multiple_of(s * LOCAL, LOCAL), LOCAL)],
            send_sem=ss1.at[j],
            recv_sem=rs1.at[j],
            device_id={"stn": to},
            device_id_type=MESH,
        )

    def stage2_copy(to):
        return pltpu.make_async_remote_copy(
            src_ref=send2.at[to],
            dst_ref=v.at[t],
            send_sem=ss2.at[to],
            recv_sem=rs2.at[t],
            device_id={"tm": to},
            device_id_type=MESH,
        )

    def bytes_of(ref, sem):
        pltpu.make_async_copy(ref, ref, sem).wait()

    filter_frames(True)
    load_table.wait()
    pl.semaphore_wait(barrier, STN - 1 + TM - 1)
    for step in range(NCH):
        j = chunk_of(lax.rem(t + 1, TM), step)
        part = jnp.dot(lhs[0 : SPILL * LOCAL, :], table[j], preferred_element_type=F32)
        halo_out[j] = part.astype(BF16)

        @pl.when(t < TM - 1)
        def _():
            halo_copy(j).start()

    filter_frames(False)

    @pl.when(t == 0)
    def _():
        halo_in[...] = jnp.zeros_like(halo_in)

    lane = lax.broadcasted_iota(jnp.int32, (1, 128), 1)

    def stage1(step):
        j = chunk_of(t, step)
        own = jnp.dot(lhs[...], table[j], preferred_element_type=F32)

        @pl.when(t > 0)
        def _():
            bytes_of(halo_in.at[j], halo_rs.at[j])

        head = own[0 : SPILL * LOCAL] + halo_in[j].astype(F32)
        own = jnp.concatenate([head, own[SPILL * LOCAL :]], axis=0)
        own = own.astype(BF16).astype(F32)
        for c in range(CH):
            for hi in range(2):
                at = (c * 2 + hi) * 128
                blocks = [own[f * LOCAL : (f + 1) * LOCAL, at : at + 128] for f in range(FRAMES)]
                for g, block in enumerate(butterfly(blocks, lane)):
                    row = (hi * 16 + g) * LOCAL
                    send1[j, row : row + LOCAL, c * 128 : (c + 1) * 128] = block.astype(BF16)
        mine = pl.ds(pl.multiple_of(s * LOCAL, LOCAL), LOCAL)
        u[j, mine, :] = send1[j, mine, :]

        @pl.loop(1, STN)
        def _(d):
            stage1_copy(j, lax.rem(s + d, STN)).start()

    def stage2(step):
        j = chunk_of(t, step)
        bytes_of(u.at[j, pl.ds(0, INPUTS - LOCAL)], rs1.at[j])
        for c in range(CH):
            block = u[j, :, c * 128 : (c + 1) * 128].astype(F32)
            low, high = block[0 : INPUTS // 2], block[INPUTS // 2 :]
            first = lane < 64
            pair = (
                jnp.where(first, low, pltpu.roll(high, 64, 1)),
                jnp.where(first, pltpu.roll(low, 64, 1), high),
            )
            for b in range(2):
                to = (j * CH + c) * 2 + b
                send2[to] = pair[b].astype(BF16)

                @pl.when(to != t)
                def _():
                    stage2_copy(to).start()

    stage1(0)
    for step in range(1, NCH):
        stage1(step)
        stage2(step - 1)
    stage2(NCH - 1)
    v[t] = send2[t]

    ref = ref_chan[0]
    ref_stn, ref_tm, ref_low = ref // 16, lax.rem(ref // 2, TM), lax.rem(ref, 2)
    row16 = lax.broadcasted_iota(jnp.int32, (2 * K, 1), 0)
    wanted = jnp.zeros((2 * K, 1), jnp.int32)
    for k in range(K):
        wanted = jnp.where(lax.rem(row16, K) == k, basis_in[k], wanted)
    column = lax.broadcasted_iota(jnp.int32, (2 * K, INPUTS), 1)
    onehot = jnp.where(column == wanted, 1.0, 0.0).astype(BF16)
    columns = jnp.zeros((2 * K, INPUTS), F32)
    here = jnp.where(s == ref_stn, 1, 0)
    for q in range(TILES):
        block = u[q // CH, :, (q % CH) * 128 : (q % CH + 1) * 128]
        picked = jnp.dot(onehot, block, preferred_element_type=F32)
        swapped = jnp.where((lane & 1) == 0, -pltpu.roll(picked, 127, 1), pltpu.roll(picked, 1, 1))
        left = jnp.where(row16 < K, picked, swapped)
        keep = (2 * q + lane // 64 == ref_tm) & (lax.rem(lane // 2, 2) == ref_low) & (here == 1)
        left = jnp.where(keep, left, 0.0).astype(BF16)
        columns = columns + lax.dot_general(
            left, block, (((1,), (1,)), ((), ())), preferred_element_type=F32
        )

    inner = lax.rem(s, 8)
    outer = s // 8

    def columns_copy(phase, d):
        if phase == 0:
            to, slot, landing, sem = {"stn": outer * 8 + lax.rem(inner + d, 8)}, inner, cols_a, crs_a
        elif phase == 1:
            to, slot, landing, sem = {"stn": lax.rem(outer + d, 4) * 8 + inner}, outer, cols_b, crs_b
        else:
            to, slot, landing, sem = {"tm": lax.rem(t + d, TM)}, t, cols_c, crs_c
        return pltpu.make_async_remote_copy(
            src_ref=cols_out.at[phase],
            dst_ref=landing.at[slot],
            send_sem=css.at[phase],
            recv_sem=sem.at[0],
            device_id=to,
            device_id_type=MESH,
        )

    for phase, (landing, sem, slot, size) in enumerate(
        ((cols_a, crs_a, inner, 8), (cols_b, crs_b, outer, 4), (cols_c, crs_c, t, TM))
    ):
        low = columns.astype(BF16)
        cols_out[phase] = low
        landing[slot] = low

        @pl.loop(1, size)
        def _(d):
            columns_copy(phase, d).start()

        bytes_of(landing.at[pl.ds(0, size - 1)], sem.at[0])
        columns = landing[0].astype(F32)
        for other in range(1, size):
            columns = columns + landing[other].astype(F32)
    columns = columns * (1.0 / SPECTRA)
    basis_re, basis_im = gram_schmidt(columns[0:K], columns[K:])
    basis[0:K, :] = basis_re
    basis[K:, :] = basis_im

    for phase, size in enumerate((8, 4, TM)):
        bytes_of(cols_a.at[pl.ds(0, size - 1)], css.at[phase])

    @pl.loop(0, NCH)
    def _(j):
        bytes_of(send1.at[j, pl.ds(0, INPUTS - LOCAL)], ss1.at[j])

    @pl.when(t < TM - 1)
    def _():
        @pl.loop(0, NCH)
        def _(j):
            bytes_of(halo_out.at[j], halo_ss.at[j])

    @pl.loop(0, TM)
    def _(other):
        @pl.when(other != t)
        def _():
            bytes_of(send2.at[other], ss2.at[other])
            bytes_of(v.at[other], rs2.at[other])


def channelise(volt, taps, table, ref_chan, basis_in):
    vmem = pl.BlockSpec(memory_space=pltpu.VMEM)
    smem = pl.BlockSpec(memory_space=pltpu.SMEM)
    dma = pltpu.SemaphoreType.DMA
    return pl.pallas_call(
        channelise_kernel,
        out_shape=(
            jax.ShapeDtypeStruct((NCH, INPUTS, WIDE), BF16),
            jax.ShapeDtypeStruct((TM, INPUTS // 2, 128), BF16),
            jax.ShapeDtypeStruct((2 * K, INPUTS), F32),
        ),
        in_specs=[vmem, vmem, pl.BlockSpec(memory_space=pl.ANY), smem, smem],
        out_specs=(vmem, vmem, vmem),
        scratch_shapes=[
            pltpu.VMEM((NCH, 2 * NFFT, 2 * WIDE), BF16),
            pltpu.VMEM((TAPS * Q, 128), F32),
            pltpu.VMEM((FRAMES * LOCAL * Q, 128), F32),
            pltpu.VMEM((FRAMES * LOCAL, 2 * NFFT), BF16),
            pltpu.VMEM((NCH, SPILL * LOCAL, 2 * WIDE), BF16),
            pltpu.VMEM((NCH, SPILL * LOCAL, 2 * WIDE), BF16),
            pltpu.VMEM((NCH, INPUTS, WIDE), BF16),
            pltpu.VMEM((TM, INPUTS // 2, 128), BF16),
            pltpu.VMEM((3, 2 * K, INPUTS), BF16),
            pltpu.VMEM((8, 2 * K, INPUTS), BF16),
            pltpu.VMEM((4, 2 * K, INPUTS), BF16),
            pltpu.VMEM((TM, 2 * K, INPUTS), BF16),
            dma,
            dma((NCH,)),
            dma((NCH,)),
            dma((NCH,)),
            dma((NCH,)),
            dma((TM,)),
            dma((TM,)),
            dma((3,)),
            dma((1,)),
            dma((1,)),
            dma((1,)),
        ],
        compiler_params=pltpu.CompilerParams(
            collective_id=0, has_side_effects=True, vmem_limit_bytes=40 * 1024 * 1024
        ),
        name="channelise",
    )(volt, taps, table, ref_chan, basis_in)


def covariance_kernel(u, v, basis, cov, proj, power):
    lane = lax.broadcasted_iota(jnp.int32, (1, 128), 1)
    lane4 = lax.broadcasted_iota(jnp.int32, (1, 512), 1)
    first = lane < 64
    tops, bottoms = [], []
    for pair in range(TM // 2):
        one, two = v[2 * pair].astype(F32), v[2 * pair + 1].astype(F32)
        tops.append(jnp.where(first, one, pltpu.roll(two, 64, 1)))
        bottoms.append(jnp.where(first, pltpu.roll(one, 64, 1), two))
    x = jnp.concatenate(
        [jnp.concatenate(tops, axis=1), jnp.concatenate(bottoms, axis=1)], axis=0
    )
    real = (lane4 & 1) == 0
    swapped = jnp.where(real, pltpu.roll(x, 511, 1), -pltpu.roll(x, 1, 1))
    x_low, swapped = x.astype(BF16), swapped.astype(BF16)
    for ch in range(2):
        keep = (lane4 & 2) == 2 * ch
        for part, left in enumerate((x_low, swapped)):
            left = jnp.where(keep, left, jnp.zeros_like(left))
            prod = lax.dot_general(
                left, x_low, (((1,), (1,)), ((), ())), preferred_element_type=F32
            )
            cov[ch, :, part * INPUTS : (part + 1) * INPUTS] = (prod * (1.0 / SPECTRA)).astype(BF16)

    b = basis[...]
    b0 = b.astype(BF16)
    rest = b - b0.astype(F32)
    b1 = rest.astype(BF16)
    b2 = (rest - b1.astype(F32)).astype(BF16)
    y = sum(jnp.dot(part, x_low, preferred_element_type=F32) for part in (b2, b1, b0))
    y_re = y[0:K] + pltpu.roll(y[K:], 511, 1)
    y_im = pltpu.roll(y[0:K], 511, 1) - y[K:]
    y = jnp.concatenate([y_re, y_im], axis=0)
    row = lax.broadcasted_iota(jnp.int32, (K, 128), 0)
    col = lax.broadcasted_iota(jnp.int32, (K, 128), 1)
    for ch in range(2):
        left = jnp.where((lane4 & 3) == 2 * ch, y, 0.0)
        gram = lax.dot_general(
            left, y, (((1,), (1,)), ((), ())), precision=HIGHEST, preferred_element_type=F32
        )
        re = gram[0:K, 0:K] + gram[K:, K:]
        im = gram[K:, 0:K] - gram[0:K, K:]
        flat = jnp.concatenate([re] * K + [im] * K, axis=1)
        flat = jnp.where(lax.rem(col // K, K) == row, flat, 0.0)
        proj[ch : ch + 1, :] = jnp.sum(flat, axis=0, keepdims=True) * (1.0 / SPECTRA)

    rows = lax.broadcasted_iota(jnp.int32, (16, 128), 0)
    lanes = lax.broadcasted_iota(jnp.int32, (16, 128), 1)
    spectrum = jnp.where(
        lax.rem(lax.broadcasted_iota(jnp.int32, (128, 16), 0) // 4, 16)
        == lax.broadcasted_iota(jnp.int32, (128, 16), 1),
        1.0,
        0.0,
    )
    total = jnp.zeros((16, 16), F32)
    for q in range(TILES):
        z = jnp.dot(b0, u[q // CH, :, (q % CH) * 128 : (q % CH + 1) * 128], preferred_element_type=F32)
        z_re = z[0:K] + pltpu.roll(z[K:], 127, 1)
        z_im = pltpu.roll(z[0:K], 127, 1) - z[K:]
        squares = jnp.sum(z_re * z_re + z_im * z_im, axis=0, keepdims=True)
        channel = (2 * q + lanes // 64) * 2 + lax.rem(lanes // 2, 2)
        keep = (channel == rows) & ((lanes & 1) == 0)
        total = total + jnp.dot(
            jnp.where(keep, squares, 0.0), spectrum, precision=HIGHEST, preferred_element_type=F32
        )
    power[...] = total


def covariance_of(u, v, basis):
    vmem = pl.BlockSpec(memory_space=pltpu.VMEM)
    return pl.pallas_call(
        covariance_kernel,
        out_shape=(
            jax.ShapeDtypeStruct((2, INPUTS, 2 * INPUTS), BF16),
            jax.ShapeDtypeStruct((2, 2 * K * K), F32),
            jax.ShapeDtypeStruct((16, FRAMES), F32),
        ),
        in_specs=[vmem] * 3,
        out_specs=(vmem,) * 3,
        compiler_params=pltpu.CompilerParams(vmem_limit_bytes=40 * 1024 * 1024),
        name="covariances",
    )(u, v, basis)


def on_device(table, voltages, filter_taps, reference_channel, basis_inputs):
    volt = voltages.reshape(LOCAL, 2, FRAMES * SUB, 128).transpose(0, 2, 1, 3).reshape(-1, 128)
    u, v, basis = channelise(volt, filter_taps, table, reference_channel, basis_inputs)
    return covariance_of(u, v, basis)


def solution(mesh):
    table = transform_table()

    def whole(voltages, filter_taps, reference_channel, basis_inputs):
        return jax.shard_map(
            on_device,
            mesh=mesh,
            in_specs=(P(), P("stn", None, "tm"), P(), P(), P()),
            out_specs=(P(("stn", "tm"), None, None), P(("stn", "tm"), None), P("stn", "tm")),
            check_vma=False,
        )(jnp.asarray(table), voltages, filter_taps, reference_channel, basis_inputs)

    return whole
```

time: 387 us -> 68.7 us (0.18)
  other arithmetic: 159 us -> 0 us
  blocking collectives: 105 us -> 0 us
  Pallas kernels: 0 us -> 61.9 us
  local copies, waits for them, and re-layouts: 61.9 us -> 5.27 us
  matrix products: 34.3 us -> 0 us
  starting transfers between devices: 9.4 us -> 0 us
  waiting for transfers between devices: 8.28 us -> 0 us
  between operations: 6.91 us -> 1.3 us
    psum x1 -> x0, blocking collectives: 74.6 us -> none  [spread(): return lax.psum(jnp.where(mine, shard, jnp.zeros_like(shard)), axis)]
    pallas_call x0 -> x2, Pallas kernels: none -> 61.9 us  [the longest x1 58.7 us: channelise(): pl.pallas_call(channelise_kernel, out_shape=(jax.ShapeDtypeStruct((NCH, I...]
    reduce_sum x15 -> x0, other arithmetic: 44.8 us -> none  [the longest x7 31.3 us: orthonormal(): inner_real = jnp.sum(q_real * vec_real + q_imag * vec_imag)]
    mul x2 -> x0, other arithmetic: 43.9 us -> none  [the longest x1 35.1 us: orthonormal(): basis_imag.append(vec_imag * inverse)]
    add x8 -> x0, other arithmetic: 36.8 us -> none  [add_block(): return total + rounded]
    dot_general x48 -> x0, matrix products: 34.3 us -> none  [the longest x8 3.9 us: block_sums(): jnp.einsum('itc,jtc->cij', part_real, part_imag, preferred_element_type=j...]
    all_to_all x1 -> x0, blocking collectives: 30 us -> none  [on_device(): lax.all_to_all(spectra, 'stn', split_axis=2, concat_axis=0, tiled=True)]
    another operation x3 -> x0, other arithmetic: 18.3 us -> none
  transfers between devices with their start and end apart: 2 -> 0, of which waited for: 1 -> 0; matrix products, arithmetic and copies ran while one was open for 9% -> 0% of each run, Pallas kernels for 0% -> 0%
where the time goes in v1:
time: 68.7 us; the launch traced here: 68.5 us
  Pallas kernels  61.9 us (90%)
  local copies, waits for them, and re-layouts  5.27 us (8%)
  between operations  1.3 us (2%)
    pallas_call x1, Pallas kernels, channelise(): pl.pallas_call(channelise_kernel, out_shape=(jax.ShapeDtypeStruct((NCH, I...  58.7 us
    unnamed x8, local copies, waits for them, and re-layouts  5.27 us
    pallas_call x1, Pallas kernels, covariance_of(): pl.pallas_call(covariance_kernel, out_shape=(jax.ShapeDtypeStruct((2, INP...  3.22 us

profile of v1, /device:TPU:1, one launch (start us, length us, event | category | flops | bytes accessed | tf_op | source)
XLA Modules:
  0.0 68.5 jit_solution(16033146872349206912)
XLA Ops:
  1.3 0.0 copy-start
  1.3 2.2 %copy-done = bf16[4,2048,256]{2,1,0:T(8,128)(2,1)S(1)} copy-done((bf16[4,2048,256]{2,1,0:T(8,128)(2,1)S(1)}, bf16[4,2048,256]{2,1,0:T(8,128)(2,1)}, u32[]{:S(2)}) %copy-start) | copy-done | bytes 4194328
  3.5 0.0 copy-start.1
  3.5 1.6 %copy-done.1 = s32[16,2,16384]{2,1,0:T(2,128)S(1)} copy-done((s32[16,2,16384]{2,1,0:T(2,128)S(1)}, s32[16,2,16384]{2,1,0:T(2,128)}, u32[]{:S(2)}) %copy-start.1) | copy-done | bytes 2097176
  5.1 0.0 copy-start.2
  5.1 0.8 %copy-done.2 = f32[16,1024]{1,0:T(8,128)S(1)} copy-done((f32[16,1024]{1,0:T(8,128)S(1)}, f32[16,1024]{1,0:T(8,128)}, u32[]{:S(2)}) %copy-start.2) | copy-done | bytes 65560
  5.9 0.0 copy-start.3
  5.9 0.7 copy-done.3
  6.6 58.7 %channelise.1 = (bf16[4,512,128]{2,1,0:T(8,128)(2,1)S(1)}, bf16[8,256,128]{2,1,0:T(8,128)(2,1)S(1)}, f32[16,512]{1,0:T(8,128)S(1)}) custom-call(s32[4096,128]{1,0:T(8,128)S(1)} %bitcast.5, f32[16,1024]{1,0:T(8,128)S(1)} %copy-done.2, bf16[4,2048,256]{2,1,0:T(8,128)(2,1)S(1)} %copy-done, s32[1]{0:T(128)S(6)} %copy.9.ref_chan, s32[8]{0:T(128)S(1)} %copy-done.3), custom_call_target="tpu_custom_call" | custom-call | tf_op jit(solution)/shard_map/channelise/pallas_call | solution.py:318
  65.2 3.2 %covariances.1 = (bf16[2,512,1024]{2,1,0:T(8,128)(2,1)}, f32[2,128]{1,0:T(2,128)}, f32[16,16]{1,0:T(8,128)}) custom-call(bf16[4,512,128]{2,1,0:T(8,128)(2,1)S(1)} %get-tuple-element.6.u, bf16[8,256,128]{2,1,0:T(8,128)(2,1)S(1)} %get-tuple-element.7.v, f32[16,512]{1,0:T(8,128)S(1)} %get-tuple-element.8.basis), custom_call_target="tpu_custom_call" | custom-call | tf_op jit(solution)/shard_map/covariances/pallas_call | solution.py:429
Async XLA Ops:
  1.3 2.2 %copy-start = (bf16[4,2048,256]{2,1,0:T(8,128)(2,1)S(1)}, bf16[4,2048,256]{2,1,0:T(8,128)(2,1)}, u32[]{:S(2)}) copy-start(bf16[4,2048,256]{2,1,0:T(8,128)(2,1)} %constant.2.clone.table_hbm) | copy-start | bytes 12582916
  3.5 1.6 %copy-start.1 = (s32[16,2,16384]{2,1,0:T(2,128)S(1)}, s32[16,2,16384]{2,1,0:T(2,128)}, u32[]{:S(2)}) copy-start(s32[16,2,16384]{2,1,0:T(2,128)} %param.5) | copy-start | bytes 6291460
  5.1 0.8 %copy-start.2 = (f32[16,1024]{1,0:T(8,128)S(1)}, f32[16,1024]{1,0:T(8,128)}, u32[]{:S(2)}) copy-start(f32[16,1024]{1,0:T(8,128)} %taps.1) | copy-start | bytes 196612
  5.9 0.7 copy-start.3

commit v2 on v1

--- a/solution.py
+++ b/solution.py
@@ -22,6 +22,10 @@
 SUB = NFFT // 128
 Q = 2 * SUB
 SPILL = TAPS - 1
+VOLT_ROWS = LOCAL * FRAMES * Q
+PACE = 1
+COLUMNS_AT = 1
+PARTS = 4
 TILES = 4
 CH = 1
 NCH = TILES // CH
@@ -78,13 +82,29 @@
 
 
 def channelise_kernel(
-    volt, taps, table_hbm, ref_chan, basis_in,
+    volt_hbm, taps_hbm, table_hbm, ref_hbm, basis_hbm,
     u, v, basis,
-    table, tap_rows, frames_f, lhs, halo_out, halo_in, send1, send2, cols_out, cols_a, cols_b, cols_c,
-    table_sem, halo_ss, halo_rs, ss1, rs1, ss2, rs2, css, crs_a, crs_b, crs_c,
+    volt, taps, ref_chan, basis_in, table, tap_rows, frames_f, lhs, halo_out, halo_in, send1, send2, ref_halo, ref_out, ref_in, cols_out, cols_in,
+    volt_sem, small_sem, table_sem, halo_ss, halo_rs, ss1, rs1, ss2, rs2, ref_sem, cols_sem,
 ):
     s = lax.axis_index("stn")
     t = lax.axis_index("tm")
+    load_taps = pltpu.make_async_copy(taps_hbm, taps, small_sem.at[0])
+    load_taps.start()
+    load_ref = pltpu.make_async_copy(ref_hbm, ref_chan, small_sem.at[1])
+    load_ref.start()
+    load_basis = pltpu.make_async_copy(basis_hbm, basis_in, small_sem.at[2])
+    load_basis.start()
+
+    def load_volt(part):
+        rows = pl.ds(pl.multiple_of(part * (VOLT_ROWS // PARTS), 8), VOLT_ROWS // PARTS)
+        return pltpu.make_async_copy(volt_hbm.at[rows], volt.at[rows], volt_sem.at[part])
+
+    for part in range(PARTS):
+        load_volt(part).start()
+    load_table = pltpu.make_async_copy(table_hbm, table, table_sem)
+    load_table.start()
+
     barrier = pltpu.get_barrier_semaphore()
 
     @pl.loop(1, STN)
@@ -95,9 +115,7 @@
     def _(d):
         pl.semaphore_signal(barrier, 1, device_id={"tm": lax.rem(t + d, TM)}, device_id_type=MESH)
 
-    load_table = pltpu.make_async_copy(table_hbm, table, table_sem)
-    load_table.start()
-
+    load_taps.wait()
     for sub in range(SUB):
         part = taps[:, sub * 128 : (sub + 1) * 128] * (1.0 / 64.0)
         for p in range(2):
@@ -106,6 +124,11 @@
     def filter_frames(spill):
         @pl.loop(0, LOCAL * 2)
         def _(step):
+            if spill:
+                @pl.when(lax.rem(step, LOCAL * 2 // PARTS) == 0)
+                def _():
+                    load_volt(step // (LOCAL * 2 // PARTS)).wait()
+
             i, half = step // 2, lax.rem(step, 2)
             base = pl.multiple_of(i * (FRAMES * Q) + half * 8, 8)
             x = [volt[pl.ds(base + f * Q, 8), :].astype(F32) for f in range(FRAMES)]
@@ -159,25 +182,108 @@
     def bytes_of(ref, sem):
         pltpu.make_async_copy(ref, ref, sem).wait()
 
+    lane = lax.broadcasted_iota(jnp.int32, (1, 128), 1)
+
+    def ref_tile(rows, ref_table):
+        part = jnp.dot(lhs[0 : rows * LOCAL, :], ref_table, preferred_element_type=F32)
+        total = jnp.zeros((LOCAL, 128), F32)
+        for f in range(rows):
+            total = total + jnp.where(
+                lax.rem(lane // 2, FRAMES) == f, part[f * LOCAL : (f + 1) * LOCAL], 0.0
+            )
+        return total
+
+    def ref_halo_copy():
+        return pltpu.make_async_remote_copy(
+            src_ref=ref_halo.at[0],
+            dst_ref=ref_halo.at[1],
+            send_sem=ref_sem.at[0],
+            recv_sem=ref_sem.at[1],
+            device_id={"tm": lax.rem(t + 1, TM)},
+            device_id_type=MESH,
+        )
+
+    def ref_copy(to):
+        return pltpu.make_async_remote_copy(
+            src_ref=ref_out,
+            dst_ref=ref_in.at[pl.ds(pl.multiple_of(s * LOCAL, LOCAL), LOCAL)],
+            send_sem=ref_sem.at[2],
+            recv_sem=ref_sem.at[3],
+            device_id={"stn": to},
+            device_id_type=MESH,
+        )
+
+    def columns_copy(to):
+        return pltpu.make_async_remote_copy(
+            src_ref=cols_out,
+            dst_ref=cols_in.at[t],
+            send_sem=cols_sem.at[0],
+            recv_sem=cols_sem.at[1],
+            device_id={"tm": to},
+            device_id_type=MESH,
+        )
+
+    def next_halo(step):
+        if step >= NCH:
+            return
+
+        @pl.when(t < TM - 1)
+        def _():
+            if step >= PACE:
+                before = chunk_of(lax.rem(t + 1, TM), step - PACE)
+                bytes_of(halo_out.at[before], halo_ss.at[before])
+            halo_copy(chunk_of(lax.rem(t + 1, TM), step)).start()
+
     filter_frames(True)
     load_table.wait()
-    pl.semaphore_wait(barrier, STN - 1 + TM - 1)
+    load_ref.wait()
+    load_basis.wait()
+    ref = ref_chan[0]
+    ref_stn, ref_tm, ref_low = ref // 16, lax.rem(ref // 2, TM), lax.rem(ref, 2)
+    ref_at = (lax.rem(ref_tm // 2, CH) * 2 + ref_stn // 16) * 128
+    ref_at = ref_at + lax.rem(ref_tm, 2) * 64 + lax.rem(ref_stn, 16) * 4 + ref_low * 2
+    chosen = lax.broadcasted_iota(jnp.int32, (2 * WIDE, 128), 0) == ref_at + (lane & 1)
+    ref_table = jnp.dot(
+        table[ref_tm // (2 * CH)],
+        jnp.where(chosen, 1.0, 0.0).astype(BF16),
+        preferred_element_type=F32,
+    ).astype(BF16)
+    ref_halo[0] = ref_tile(SPILL, ref_table).astype(BF16)
     for step in range(NCH):
         j = chunk_of(lax.rem(t + 1, TM), step)
         part = jnp.dot(lhs[0 : SPILL * LOCAL, :], table[j], preferred_element_type=F32)
         halo_out[j] = part.astype(BF16)
 
-        @pl.when(t < TM - 1)
-        def _():
-            halo_copy(j).start()
+    pl.semaphore_wait(barrier, STN - 1 + TM - 1)
+
+    @pl.when(t < TM - 1)
+    def _():
+        ref_halo_copy().start()
+
+    for step in range(PACE):
+        next_halo(step)
 
     filter_frames(False)
 
     @pl.when(t == 0)
     def _():
         halo_in[...] = jnp.zeros_like(halo_in)
-
-    lane = lax.broadcasted_iota(jnp.int32, (1, 128), 1)
+        ref_halo[1] = jnp.zeros((LOCAL, 128), BF16)
+
+    own_ref = ref_tile(FRAMES, ref_table)
+
+    @pl.when(t > 0)
+    def _():
+        bytes_of(ref_halo.at[1], ref_sem.at[1])
+
+    ref_out[...] = (own_ref + ref_halo[1].astype(F32)).astype(BF16)
+    ref_in[pl.ds(pl.multiple_of(s * LOCAL, LOCAL), LOCAL), :] = ref_out[...]
+
+    @pl.loop(1, STN)
+    def _(d):
+        ref_copy(lax.rem(s + d, STN)).start()
+
+    next_halo(PACE)
 
     def stage1(step):
         j = chunk_of(t, step)
@@ -223,75 +329,52 @@
                 def _():
                     stage2_copy(to).start()
 
-    stage1(0)
-    for step in range(1, NCH):
-        stage1(step)
-        stage2(step - 1)
-    stage2(NCH - 1)
-    v[t] = send2[t]
-
-    ref = ref_chan[0]
-    ref_stn, ref_tm, ref_low = ref // 16, lax.rem(ref // 2, TM), lax.rem(ref, 2)
-    row16 = lax.broadcasted_iota(jnp.int32, (2 * K, 1), 0)
-    wanted = jnp.zeros((2 * K, 1), jnp.int32)
-    for k in range(K):
-        wanted = jnp.where(lax.rem(row16, K) == k, basis_in[k], wanted)
-    column = lax.broadcasted_iota(jnp.int32, (2 * K, INPUTS), 1)
-    onehot = jnp.where(column == wanted, 1.0, 0.0).astype(BF16)
-    columns = jnp.zeros((2 * K, INPUTS), F32)
-    here = jnp.where(s == ref_stn, 1, 0)
-    for q in range(TILES):
-        block = u[q // CH, :, (q % CH) * 128 : (q % CH + 1) * 128]
+    def send_columns():
+        bytes_of(ref_in.at[pl.ds(0, INPUTS - LOCAL)], ref_sem.at[3])
+        row16 = lax.broadcasted_iota(jnp.int32, (2 * K, 1), 0)
+        wanted = jnp.zeros((2 * K, 1), jnp.int32)
+        for k in range(K):
+            wanted = jnp.where(lax.rem(row16, K) == k, basis_in[k], wanted)
+        column = lax.broadcasted_iota(jnp.int32, (2 * K, INPUTS), 1)
+        onehot = jnp.where(column == wanted, 1.0, 0.0).astype(BF16)
+        block = ref_in[...]
         picked = jnp.dot(onehot, block, preferred_element_type=F32)
         swapped = jnp.where((lane & 1) == 0, -pltpu.roll(picked, 127, 1), pltpu.roll(picked, 1, 1))
         left = jnp.where(row16 < K, picked, swapped)
-        keep = (2 * q + lane // 64 == ref_tm) & (lax.rem(lane // 2, 2) == ref_low) & (here == 1)
-        left = jnp.where(keep, left, 0.0).astype(BF16)
-        columns = columns + lax.dot_general(
+        left = jnp.where(lane < 2 * FRAMES, left, 0.0).astype(BF16)
+        columns = lax.dot_general(
             left, block, (((1,), (1,)), ((), ())), preferred_element_type=F32
-        )
-
-    inner = lax.rem(s, 8)
-    outer = s // 8
-
-    def columns_copy(phase, d):
-        if phase == 0:
-            to, slot, landing, sem = {"stn": outer * 8 + lax.rem(inner + d, 8)}, inner, cols_a, crs_a
-        elif phase == 1:
-            to, slot, landing, sem = {"stn": lax.rem(outer + d, 4) * 8 + inner}, outer, cols_b, crs_b
-        else:
-            to, slot, landing, sem = {"tm": lax.rem(t + d, TM)}, t, cols_c, crs_c
-        return pltpu.make_async_remote_copy(
-            src_ref=cols_out.at[phase],
-            dst_ref=landing.at[slot],
-            send_sem=css.at[phase],
-            recv_sem=sem.at[0],
-            device_id=to,
-            device_id_type=MESH,
-        )
-
-    for phase, (landing, sem, slot, size) in enumerate(
-        ((cols_a, crs_a, inner, 8), (cols_b, crs_b, outer, 4), (cols_c, crs_c, t, TM))
-    ):
-        low = columns.astype(BF16)
-        cols_out[phase] = low
-        landing[slot] = low
-
-        @pl.loop(1, size)
+        ).astype(BF16)
+        cols_out[...] = columns
+        cols_in[t] = columns
+
+        @pl.loop(1, TM)
         def _(d):
-            columns_copy(phase, d).start()
-
-        bytes_of(landing.at[pl.ds(0, size - 1)], sem.at[0])
-        columns = landing[0].astype(F32)
-        for other in range(1, size):
-            columns = columns + landing[other].astype(F32)
-    columns = columns * (1.0 / SPECTRA)
-    basis_re, basis_im = gram_schmidt(columns[0:K], columns[K:])
-    basis[0:K, :] = basis_re
-    basis[K:, :] = basis_im
-
-    for phase, size in enumerate((8, 4, TM)):
-        bytes_of(cols_a.at[pl.ds(0, size - 1)], css.at[phase])
+            columns_copy(lax.rem(t + d, TM)).start()
+
+    def find_basis():
+        bytes_of(cols_in.at[pl.ds(0, TM - 1)], cols_sem.at[1])
+        columns = cols_in[0].astype(F32)
+        for other in range(1, TM):
+            columns = columns + cols_in[other].astype(F32)
+        columns = columns * (1.0 / SPECTRA)
+        basis_re, basis_im = gram_schmidt(columns[0:K], columns[K:])
+        basis[0:K, :] = basis_re
+        basis[K:, :] = basis_im
+
+    for step in range(NCH):
+        stage1(step)
+        next_halo(PACE + 1 + step)
+        if step > 0:
+            stage2(step - 1)
+        if step == COLUMNS_AT:
+            send_columns()
+    find_basis()
+    stage2(NCH - 1)
+    v[t] = send2[t]
+
+    bytes_of(cols_in.at[pl.ds(0, TM - 1)], cols_sem.at[0])
+    bytes_of(ref_in.at[pl.ds(0, INPUTS - LOCAL)], ref_sem.at[2])
 
     @pl.loop(0, NCH)
     def _(j):
@@ -299,8 +382,9 @@
 
     @pl.when(t < TM - 1)
     def _():
-        @pl.loop(0, NCH)
-        def _(j):
+        bytes_of(ref_halo.at[0], ref_sem.at[0])
+        for step in range(NCH - PACE, NCH):
+            j = chunk_of(lax.rem(t + 1, TM), step)
             bytes_of(halo_out.at[j], halo_ss.at[j])
 
     @pl.loop(0, TM)
@@ -313,7 +397,7 @@
 
 def channelise(volt, taps, table, ref_chan, basis_in):
     vmem = pl.BlockSpec(memory_space=pltpu.VMEM)
-    smem = pl.BlockSpec(memory_space=pltpu.SMEM)
+    hbm = pl.BlockSpec(memory_space=pltpu.HBM)
     dma = pltpu.SemaphoreType.DMA
     return pl.pallas_call(
         channelise_kernel,
@@ -322,9 +406,13 @@
             jax.ShapeDtypeStruct((TM, INPUTS // 2, 128), BF16),
             jax.ShapeDtypeStruct((2 * K, INPUTS), F32),
         ),
-        in_specs=[vmem, vmem, pl.BlockSpec(memory_space=pl.ANY), smem, smem],
+        in_specs=[hbm] * 5,
         out_specs=(vmem, vmem, vmem),
         scratch_shapes=[
+            pltpu.VMEM((VOLT_ROWS, 128), jnp.int32),
+            pltpu.VMEM((TAPS, NFFT), F32),
+            pltpu.SMEM((1,), jnp.int32),
+            pltpu.SMEM((K,), jnp.int32),
             pltpu.VMEM((NCH, 2 * NFFT, 2 * WIDE), BF16),
             pltpu.VMEM((TAPS * Q, 128), F32),
             pltpu.VMEM((FRAMES * LOCAL * Q, 128), F32),
@@ -333,10 +421,13 @@
             pltpu.VMEM((NCH, SPILL * LOCAL, 2 * WIDE), BF16),
             pltpu.VMEM((NCH, INPUTS, WIDE), BF16),
             pltpu.VMEM((TM, INPUTS // 2, 128), BF16),
-            pltpu.VMEM((3, 2 * K, INPUTS), BF16),
-            pltpu.VMEM((8, 2 * K, INPUTS), BF16),
-            pltpu.VMEM((4, 2 * K, INPUTS), BF16),
+            pltpu.VMEM((2, LOCAL, 128), BF16),
+            pltpu.VMEM((LOCAL, 128), BF16),
+            pltpu.VMEM((INPUTS, 128), BF16),
+            pltpu.VMEM((2 * K, INPUTS), BF16),
             pltpu.VMEM((TM, 2 * K, INPUTS), BF16),
+            dma((PARTS,)),
+            dma((3,)),
             dma,
             dma((NCH,)),
             dma((NCH,)),
@@ -344,10 +435,8 @@
             dma((NCH,)),
             dma((TM,)),
             dma((TM,)),
-            dma((3,)),
-            dma((1,)),
-            dma((1,)),
-            dma((1,)),
+            dma((4,)),
+            dma((2,)),
         ],
         compiler_params=pltpu.CompilerParams(
             collective_id=0, has_side_effects=True, vmem_limit_bytes=40 * 1024 * 1024

time: 68.7 us -> 60.9 us (0.89)
  the two profiles are of different devices: /device:TPU:1 before, /device:TPU:4 now
where the time goes in v2:
time: 60.9 us; the launch traced here: 60.7 us
  Pallas kernels  54.2 us (89%)
  local copies, waits for them, and re-layouts  5.27 us (9%)
  between operations  1.3 us (2%)
    pallas_call x1, Pallas kernels, channelise(): pl.pallas_call(channelise_kernel, out_shape=(jax.ShapeDtypeStruct((NCH, I...  50.9 us
    unnamed x8, local copies, waits for them, and re-layouts  5.27 us
    pallas_call x1, Pallas kernels, covariance_of(): pl.pallas_call(covariance_kernel, out_shape=(jax.ShapeDtypeStruct((2, INP...  3.24 us

profile of v2, /device:TPU:4, one launch (start us, length us, event | category | flops | bytes accessed | tf_op | source)
XLA Modules:
  0.0 60.7 jit_solution(13225340050555270888)
XLA Ops:
  1.3 0.0 copy-start
  1.3 2.2 %copy-done = bf16[4,2048,256]{2,1,0:T(8,128)(2,1)S(1)} copy-done((bf16[4,2048,256]{2,1,0:T(8,128)(2,1)S(1)}, bf16[4,2048,256]{2,1,0:T(8,128)(2,1)}, u32[]{:S(2)}) %copy-start) | copy-done | bytes 4194328
  3.5 0.0 copy-start.1
  3.5 1.6 %copy-done.1 = s32[16,2,16384]{2,1,0:T(2,128)S(1)} copy-done((s32[16,2,16384]{2,1,0:T(2,128)S(1)}, s32[16,2,16384]{2,1,0:T(2,128)}, u32[]{:S(2)}) %copy-start.1) | copy-done | bytes 2097176
  5.1 0.0 copy-start.2
  5.1 0.8 %copy-done.2 = f32[16,1024]{1,0:T(8,128)S(1)} copy-done((f32[16,1024]{1,0:T(8,128)S(1)}, f32[16,1024]{1,0:T(8,128)}, u32[]{:S(2)}) %copy-start.2) | copy-done | bytes 65560
  5.9 0.0 copy-start.3
  5.9 0.7 %copy-done.3 = s32[8]{0:T(128)S(1)} copy-done((s32[8]{0:T(128)S(1)}, s32[8]{0:T(128)}, u32[]{:S(2)}) %copy-start.3) | copy-done | bytes 56
  6.6 50.9 %channelise.1 = (bf16[4,512,128]{2,1,0:T(8,128)(2,1)S(1)}, bf16[8,256,128]{2,1,0:T(8,128)(2,1)S(1)}, f32[16,512]{1,0:T(8,128)S(1)}) custom-call(s32[4096,128]{1,0:T(8,128)S(1)} %bitcast.5, f32[16,1024]{1,0:T(8,128)S(1)} %copy-done.2, bf16[4,2048,256]{2,1,0:T(8,128)(2,1)S(1)} %copy-done, s32[1]{0:T(128)S(6)} %copy.9.ref_hbm, s32[8]{0:T(128)S(1)} %copy-done.3), custom_call_target="tpu_custom_call" | custom-call | tf_op jit(solution)/shard_map/channelise/pallas_call | solution.py:402
  57.5 3.2 %covariances.1 = (bf16[2,512,1024]{2,1,0:T(8,128)(2,1)}, f32[2,128]{1,0:T(2,128)}, f32[16,16]{1,0:T(8,128)}) custom-call(bf16[4,512,128]{2,1,0:T(8,128)(2,1)S(1)} %get-tuple-element.6.u, bf16[8,256,128]{2,1,0:T(8,128)(2,1)S(1)} %get-tuple-element.7.v, f32[16,512]{1,0:T(8,128)S(1)} %get-tuple-element.8.basis), custom_call_target="tpu_custom_call" | custom-call | tf_op jit(solution)/shard_map/covariances/pallas_call | solution.py:518
Async XLA Ops:
  1.3 2.2 %copy-start = (bf16[4,2048,256]{2,1,0:T(8,128)(2,1)S(1)}, bf16[4,2048,256]{2,1,0:T(8,128)(2,1)}, u32[]{:S(2)}) copy-start(bf16[4,2048,256]{2,1,0:T(8,128)(2,1)} %constant.2.clone.table_hbm) | copy-start | bytes 12582916
  3.5 1.6 %copy-start.1 = (s32[16,2,16384]{2,1,0:T(2,128)S(1)}, s32[16,2,16384]{2,1,0:T(2,128)}, u32[]{:S(2)}) copy-start(s32[16,2,16384]{2,1,0:T(2,128)} %param.5) | copy-start | bytes 6291460
  5.1 0.8 %copy-start.2 = (f32[16,1024]{1,0:T(8,128)S(1)}, f32[16,1024]{1,0:T(8,128)}, u32[]{:S(2)}) copy-start(f32[16,1024]{1,0:T(8,128)} %taps_hbm.1) | copy-start | bytes 196612
  5.9 0.7 %copy-start.3 = (s32[8]{0:T(128)S(1)}, s32[8]{0:T(128)}, u32[]{:S(2)}) copy-start(s32[8]{0:T(128)} %basis_hbm.1) | copy-start | bytes 100

commit v3 on v2

v3 whole, which is shorter than its diff:
```python
import functools
import math

import jax
import jax.numpy as jnp
import numpy as np
from jax import lax
from jax.experimental import pallas as pl
from jax.experimental.pallas import tpu as pltpu
from jax.sharding import PartitionSpec as P

NFFT = 1024
FCH = 512
TAPS = 16
K = 8
INPUTS = 512
SPECTRA = 128
STN = 32
TM = 8
LOCAL = INPUTS // STN
FRAMES = SPECTRA // TM
SUB = NFFT // 128
Q = 2 * SUB
SPILL = TAPS - 1
VOLT_ROWS = LOCAL * FRAMES * Q
COLUMNS_AT = 1
PARTS = 4
PIECES = 4
TILES = TM // 2
OWN_ROWS, SPILL_ROWS = FRAMES * LOCAL, SPILL * LOCAL
LIMIT = 60
MESH = pl.DeviceIdType.MESH
F32 = jnp.float32
BF16 = jnp.bfloat16
HIGHEST = lax.Precision.HIGHEST


def transform_table():
    phase = np.arange(NFFT)[:, None] * np.arange(FCH)[None, :] % NFFT
    angle = phase.astype(np.float32) * np.float32(2.0 * math.pi / NFFT)
    factor = np.float32(1.0 / math.sqrt(NFFT))
    cosine, sine = np.cos(angle) * factor, np.sin(angle) * factor
    table_re = np.stack([cosine, -sine], axis=2)
    table_im = np.stack([sine, cosine], axis=2)
    both = np.stack([table_re.reshape(SUB, 128, FCH, 2), table_im.reshape(SUB, 128, FCH, 2)], axis=1)
    both = both.reshape(2 * NFFT, STN, PIECES, 2, 2, 2)
    both = both.transpose(2, 0, 3, 1, 4, 5)
    return both.reshape(PIECES, 2 * NFFT, 256).astype(jnp.bfloat16)


def butterfly(blocks, lane):
    blocks = list(blocks)
    for bit in range(5):
        step, shift = 1 << bit, 4 << bit
        low = (lane & shift) == 0
        for a in range(32):
            if a & step:
                continue
            first, second = blocks[a], blocks[a | step]
            blocks[a] = jnp.where(low, first, pltpu.roll(second, shift, 1))
            blocks[a | step] = jnp.where(low, pltpu.roll(first, 128 - shift, 1), second)
    return blocks


def gram_schmidt(vec_re, vec_im):
    row = lax.broadcasted_iota(jnp.int32, (K, 1), 0)
    for k in range(K):
        w_re, w_im = vec_re[k : k + 1], vec_im[k : k + 1]
        in_re = jnp.sum(w_re * vec_re + w_im * vec_im, axis=1, keepdims=True)
        in_im = jnp.sum(w_re * vec_im - w_im * vec_re, axis=1, keepdims=True)
        inverse = lax.rsqrt(in_re[k : k + 1] + 1e-06)
        q_re, q_im = w_re * inverse, w_im * inverse
        c_re = jnp.where(row > k, in_re * inverse, 0.0)
        c_im = jnp.where(row > k, in_im * inverse, 0.0)
        new_re = vec_re - (q_re * c_re - q_im * c_im)
        new_im = vec_im - (q_re * c_im + q_im * c_re)
        vec_re = jnp.where(row == k, q_re, new_re)
        vec_im = jnp.where(row == k, q_im, new_im)
    return vec_re, vec_im


def covariances(v, basis, cov, proj):
    lane4 = lax.broadcasted_iota(jnp.int32, (1, 512), 1)
    x = jnp.concatenate([v[m].astype(F32) for m in range(TILES)], axis=1)
    real = (lane4 & 1) == 0
    swapped = jnp.where(real, pltpu.roll(x, 511, 1), -pltpu.roll(x, 1, 1))
    x_low, swapped = x.astype(BF16), swapped.astype(BF16)
    for ch in range(2):
        keep = (lane4 & 2) == 2 * ch
        for part, left in enumerate((x_low, swapped)):
            left = jnp.where(keep, left, jnp.zeros_like(left))
            prod = lax.dot_general(
                left, x_low, (((1,), (1,)), ((), ())), preferred_element_type=F32
            )
            cov[ch, :, part * INPUTS : (part + 1) * INPUTS] = (prod * (1.0 / SPECTRA)).astype(BF16)

    b = basis[...]
    b0 = b.astype(BF16)
    rest = b - b0.astype(F32)
    b1 = rest.astype(BF16)
    b2 = (rest - b1.astype(F32)).astype(BF16)
    y = sum(jnp.dot(part, x_low, preferred_element_type=F32) for part in (b2, b1, b0))
    y_re = y[0:K] + pltpu.roll(y[K:], 511, 1)
    y_im = pltpu.roll(y[0:K], 511, 1) - y[K:]
    y = jnp.concatenate([y_re, y_im], axis=0)
    row = lax.broadcasted_iota(jnp.int32, (K, 128), 0)
    col = lax.broadcasted_iota(jnp.int32, (K, 128), 1)
    for ch in range(2):
        left = jnp.where((lane4 & 3) == 2 * ch, y, 0.0)
        gram = lax.dot_general(
            left, y, (((1,), (1,)), ((), ())), precision=HIGHEST, preferred_element_type=F32
        )
        re = gram[0:K, 0:K] + gram[K:, K:]
        im = gram[K:, 0:K] - gram[0:K, K:]
        flat = jnp.concatenate([re] * K + [im] * K, axis=1)
        flat = jnp.where(lax.rem(col // K, K) == row, flat, 0.0)
        proj[ch : ch + 1, :] = jnp.sum(flat, axis=0, keepdims=True) * (1.0 / SPECTRA)


def channelise_kernel(
    volt_hbm, taps_hbm, table_hbm, ref_hbm, basis_hbm,
    cov, proj, power,
    volt, taps, ref_chan, basis_in, table, tap_rows, frames_f, lhs, spill_out, spill_in, own_out, own_in,
    v, basis, send1, ref_halo, ref_out, ref_in, cols_out, cols_in, pow_out, pow_in,
    volt_sem, small_sem, table_sem, spill_ss, spill_rs, own_ss, own_rs, ss1, rs1, ref_sem, cols_sem, pow_ss, pow_rs,
):
    s = lax.axis_index("stn")
    t = lax.axis_index("tm")
    load_taps = pltpu.make_async_copy(taps_hbm, taps, small_sem.at[0])
    load_taps.start()
    load_ref = pltpu.make_async_copy(ref_hbm, ref_chan, small_sem.at[1])
    load_ref.start()
    load_basis = pltpu.make_async_copy(basis_hbm, basis_in, small_sem.at[2])
    load_basis.start()

    def load_volt(part):
        rows = pl.ds(pl.multiple_of(part * (VOLT_ROWS // PARTS), 8), VOLT_ROWS // PARTS)
        return pltpu.make_async_copy(volt_hbm.at[rows], volt.at[rows], volt_sem.at[part])

    for part in range(PARTS):
        load_volt(part).start()
    load_table = pltpu.make_async_copy(table_hbm, table, table_sem)
    load_table.start()

    barrier = pltpu.get_barrier_semaphore()

    @pl.loop(1, STN)
    def _(d):
        pl.semaphore_signal(barrier, 1, device_id={"stn": lax.rem(s + d, STN)}, device_id_type=MESH)

    @pl.loop(1, TM)
    def _(d):
        pl.semaphore_signal(barrier, 1, device_id={"tm": lax.rem(t + d, TM)}, device_id_type=MESH)

    load_taps.wait()
    for sub in range(SUB):
        part = taps[:, sub * 128 : (sub + 1) * 128] * (1.0 / 64.0)
        for p in range(2):
            tap_rows[pl.ds(sub * 2 + p, TAPS, stride=Q), :] = part

    def filter_frames(spill):
        @pl.loop(0, LOCAL * 2)
        def _(step):
            if spill:
                @pl.when(lax.rem(step, LOCAL * 2 // PARTS) == 0)
                def _():
                    load_volt(step // (LOCAL * 2 // PARTS)).wait()

            i, half = step // 2, lax.rem(step, 2)
            base = pl.multiple_of(i * (FRAMES * Q) + half * 8, 8)
            x = [volt[pl.ds(base + f * Q, 8), :].astype(F32) for f in range(FRAMES)]
            tap = [tap_rows[pl.ds(pl.multiple_of(k * Q + half * 8, 8), 8), :] for k in range(TAPS)]
            for f in range(SPILL if spill else FRAMES):
                acc = None
                for j in range(f + 1, FRAMES) if spill else range(f + 1):
                    k = j - f - 1 if spill else SPILL - f + j
                    term = tap[k] * x[j]
                    acc = term if acc is None else acc + term
                row = pl.multiple_of((f * LOCAL + i) * Q + half * 8, 8)
                frames_f[pl.ds(row, 8), :] = acc

        rows = (SPILL if spill else FRAMES) * LOCAL
        for q in range(Q):
            lhs[0:rows, q * 128 : (q + 1) * 128] = frames_f[pl.ds(q, rows, stride=Q), :].astype(BF16)

    def spill_copy(to):
        return pltpu.make_async_remote_copy(
            src_ref=spill_out.at[to],
            dst_ref=spill_in.at[lax.rem(t + 1, TM)],
            send_sem=spill_ss,
            recv_sem=spill_rs.at[lax.rem(t + 1, TM)],
            device_id={"tm": to},
            device_id_type=MESH,
        )

    def own_copy(to):
        return pltpu.make_async_remote_copy(
            src_ref=own_out.at[to],
            dst_ref=own_in.at[t],
            send_sem=own_ss,
            recv_sem=own_rs.at[t],
            device_id={"tm": to},
            device_id_type=MESH,
        )

    def turn_copy(m, to):
        return pltpu.make_async_remote_copy(
            src_ref=send1.at[m, pl.ds(pl.multiple_of(to * LOCAL, LOCAL), LOCAL)],
            dst_ref=v.at[m, pl.ds(pl.multiple_of(s * LOCAL, LOCAL), LOCAL)],
            send_sem=ss1.at[m],
            recv_sem=rs1.at[m],
            device_id={"stn": to},
            device_id_type=MESH,
        )

    def power_copy(to):
        return pltpu.make_async_remote_copy(
            src_ref=pow_out.at[to],
            dst_ref=pow_in.at[t],
            send_sem=pow_ss,
            recv_sem=pow_rs,
            device_id={"tm": to},
            device_id_type=MESH,
        )

    def bytes_of(ref, sem):
        pltpu.make_async_copy(ref, ref, sem).wait()

    lane = lax.broadcasted_iota(jnp.int32, (1, 128), 1)

    def ref_tile(rows, ref_table):
        part = jnp.dot(lhs[0 : rows * LOCAL, :], ref_table, preferred_element_type=F32)
        total = jnp.zeros((LOCAL, 128), F32)
        for f in range(rows):
            total = total + jnp.where(
                lax.rem(lane // 2, FRAMES) == f, part[f * LOCAL : (f + 1) * LOCAL], 0.0
            )
        return total

    def ref_halo_copy():
        return pltpu.make_async_remote_copy(
            src_ref=ref_halo.at[0],
            dst_ref=ref_halo.at[1],
            send_sem=ref_sem.at[0],
            recv_sem=ref_sem.at[1],
            device_id={"tm": lax.rem(t + 1, TM)},
            device_id_type=MESH,
        )

    def ref_copy(to):
        return pltpu.make_async_remote_copy(
            src_ref=ref_out,
            dst_ref=ref_in.at[pl.ds(pl.multiple_of(s * LOCAL, LOCAL), LOCAL)],
            send_sem=ref_sem.at[2],
            recv_sem=ref_sem.at[3],
            device_id={"stn": to},
            device_id_type=MESH,
        )

    def columns_copy(to):
        return pltpu.make_async_remote_copy(
            src_ref=cols_out,
            dst_ref=cols_in.at[t],
            send_sem=cols_sem.at[0],
            recv_sem=cols_sem.at[1],
            device_id={"tm": to},
            device_id_type=MESH,
        )

    filter_frames(True)
    load_table.wait()
    load_ref.wait()
    load_basis.wait()
    ref = ref_chan[0]
    ref_stn, ref_tm, ref_low = ref // 16, lax.rem(ref // 2, TM), lax.rem(ref, 2)
    ref_at = lax.rem(ref_tm, 2) * 128 + ref_stn * 4 + ref_low * 2
    chosen = lax.broadcasted_iota(jnp.int32, (256, 128), 0) == ref_at + (lane & 1)
    ref_table = jnp.dot(
        table[ref_tm // 2],
        jnp.where(chosen, 1.0, 0.0).astype(BF16),
        preferred_element_type=F32,
    ).astype(BF16)
    ref_halo[0] = ref_tile(SPILL, ref_table).astype(BF16)
    for piece in range(PIECES):
        part = jnp.dot(lhs[0:SPILL_ROWS, :], table[piece], preferred_element_type=F32).astype(BF16)
        spill_out[2 * piece] = part[:, 0:128]
        spill_out[2 * piece + 1] = part[:, 128:]

    @pl.when(t < TM - 1)
    def _():
        spill_in[t + 1] = spill_out[t]

    spill_in[0] = jnp.zeros((SPILL_ROWS, 128), BF16)

    pl.semaphore_wait(barrier, STN - 1 + TM - 1)

    @pl.when(t < TM - 1)
    def _():
        ref_halo_copy().start()

        @pl.loop(1, TM)
        def _(d):
            spill_copy(lax.rem(t + d, TM)).start()

    filter_frames(False)

    for step in range(PIECES):
        piece = lax.rem(t // 2 + 1 + step, PIECES)
        part = jnp.dot(lhs[...], table[piece], preferred_element_type=F32).astype(BF16)
        for b in range(2):
            to = 2 * piece + b
            own_out[to] = part[:, b * 128 : (b + 1) * 128]

            @pl.when(to != t)
            def _():
                own_copy(to).start()

    own_in[t] = own_out[t]

    @pl.when(t == 0)
    def _():
        ref_halo[1] = jnp.zeros((LOCAL, 128), BF16)

    own_ref = ref_tile(FRAMES, ref_table)

    @pl.when(t > 0)
    def _():
        bytes_of(ref_halo.at[1], ref_sem.at[1])

    ref_out[...] = (own_ref + ref_halo[1].astype(F32)).astype(BF16)
    ref_in[pl.ds(pl.multiple_of(s * LOCAL, LOCAL), LOCAL), :] = ref_out[...]

    @pl.loop(1, STN)
    def _(d):
        ref_copy(lax.rem(s + d, STN)).start()

    def turn(step):
        m = lax.rem(t // 2 + step, TILES)
        blocks = []
        for b in range(2):
            block = 2 * m + b

            @pl.when(block != t)
            def _():
                bytes_of(own_in.at[block], own_rs.at[block])

            @pl.when((block != 0) & (block != t + 1))
            def _():
                bytes_of(spill_in.at[block], spill_rs.at[block])

            own = own_in[block].astype(F32)
            head = own[0:SPILL_ROWS] + spill_in[block].astype(F32)
            own = jnp.concatenate([head, own[SPILL_ROWS:]], axis=0).astype(BF16).astype(F32)
            blocks += [own[f * LOCAL : (f + 1) * LOCAL] for f in range(FRAMES)]
        for to, block in enumerate(butterfly(blocks, lane)):
            send1[m, to * LOCAL : (to + 1) * LOCAL, :] = block.astype(BF16)
        mine = pl.ds(pl.multiple_of(s * LOCAL, LOCAL), LOCAL)
        v[m, mine, :] = send1[m, mine, :]

        @pl.loop(1, STN)
        def _(d):
            turn_copy(m, lax.rem(s + d, STN)).start()

    def send_columns():
        bytes_of(ref_in.at[pl.ds(0, INPUTS - LOCAL)], ref_sem.at[3])
        row16 = lax.broadcasted_iota(jnp.int32, (2 * K, 1), 0)
        wanted = jnp.zeros((2 * K, 1), jnp.int32)
        for k in range(K):
            wanted = jnp.where(lax.rem(row16, K) == k, basis_in[k], wanted)
        column = lax.broadcasted_iota(jnp.int32, (2 * K, INPUTS), 1)
        onehot = jnp.where(column == wanted, 1.0, 0.0).astype(BF16)
        block = ref_in[...]
        picked = jnp.dot(onehot, block, preferred_element_type=F32)
        swapped = jnp.where((lane & 1) == 0, -pltpu.roll(picked, 127, 1), pltpu.roll(picked, 1, 1))
        left = jnp.where(row16 < K, picked, swapped)
        left = jnp.where(lane < 2 * FRAMES, left, 0.0).astype(BF16)
        columns = lax.dot_general(
            left, block, (((1,), (1,)), ((), ())), preferred_element_type=F32
        ).astype(BF16)
        cols_out[...] = columns
        cols_in[t] = columns

        @pl.loop(1, TM)
        def _(d):
            columns_copy(lax.rem(t + d, TM)).start()

    def find_basis():
        bytes_of(cols_in.at[pl.ds(0, TM - 1)], cols_sem.at[1])
        columns = cols_in[0].astype(F32)
        for other in range(1, TM):
            columns = columns + cols_in[other].astype(F32)
        columns = columns * (1.0 / SPECTRA)
        basis_re, basis_im = gram_schmidt(columns[0:K], columns[K:])
        basis[0:K, :] = basis_re
        basis[K:, :] = basis_im

    for step in range(TILES):
        turn(step)
        if step == COLUMNS_AT:
            send_columns()
    find_basis()

    low = basis[...].astype(BF16)
    rows16 = lax.broadcasted_iota(jnp.int32, (16, 128), 0)
    lanes16 = lax.broadcasted_iota(jnp.int32, (16, 128), 1)
    keep = (lanes16 // 64 == rows16 // 8) & (lax.rem(lanes16, 4) == 2 * lax.rem(rows16, 8))
    spectrum = jnp.where(
        lax.rem(lax.broadcasted_iota(jnp.int32, (128, 128), 0) // 4, FRAMES)
        == lax.broadcasted_iota(jnp.int32, (128, 128), 1),
        1.0,
        0.0,
    )
    for step in range(TILES):
        m = lax.rem(t // 2 + step, TILES)
        bytes_of(v.at[m, pl.ds(0, INPUTS - LOCAL)], rs1.at[m])
        z = jnp.dot(low, v[m], preferred_element_type=F32)
        z_re = z[0:K] + pltpu.roll(z[K:], 127, 1)
        z_im = pltpu.roll(z[0:K], 127, 1) - z[K:]
        squares = jnp.sum(z_re * z_re + z_im * z_im, axis=0, keepdims=True)
        both = jnp.dot(
            jnp.where(keep, squares, 0.0), spectrum, precision=HIGHEST, preferred_element_type=F32
        )
        pow_out[2 * m] = both[0:8]
        pow_out[2 * m + 1] = both[8:16]
    pow_in[t] = pow_out[t]

    @pl.loop(1, TM)
    def _(d):
        power_copy(lax.rem(t + d, TM)).start()

    covariances(v, basis, cov, proj)

    bytes_of(pow_in.at[pl.ds(0, TM - 1)], pow_rs)
    for owner in range(TM):
        power[2 * owner : 2 * owner + 2, :] = pow_in[owner, 0:2, 0:FRAMES]

    bytes_of(cols_in.at[pl.ds(0, TM - 1)], cols_sem.at[0])
    bytes_of(ref_in.at[pl.ds(0, INPUTS - LOCAL)], ref_sem.at[2])

    bytes_of(pow_out.at[pl.ds(0, TM - 1)], pow_ss)
    bytes_of(own_out.at[pl.ds(0, TM - 1)], own_ss)

    @pl.loop(0, TILES)
    def _(m):
        bytes_of(send1.at[m, pl.ds(0, INPUTS - LOCAL)], ss1.at[m])

    @pl.when(t < TM - 1)
    def _():
        bytes_of(ref_halo.at[0], ref_sem.at[0])
        bytes_of(spill_out.at[pl.ds(0, TM - 1)], spill_ss)


def channelise(volt, taps, table, ref_chan, basis_in):
    vmem = pl.BlockSpec(memory_space=pltpu.VMEM)
    hbm = pl.BlockSpec(memory_space=pltpu.HBM)
    dma = pltpu.SemaphoreType.DMA
    return pl.pallas_call(
        channelise_kernel,
        out_shape=(
            jax.ShapeDtypeStruct((2, INPUTS, 2 * INPUTS), BF16),
            jax.ShapeDtypeStruct((2, 2 * K * K), F32),
            jax.ShapeDtypeStruct((16, FRAMES), F32),
        ),
        in_specs=[hbm] * 5,
        out_specs=(vmem, vmem, vmem),
        scratch_shapes=[
            pltpu.VMEM((VOLT_ROWS, 128), jnp.int32),
            pltpu.VMEM((TAPS, NFFT), F32),
            pltpu.SMEM((1,), jnp.int32),
            pltpu.SMEM((K,), jnp.int32),
            pltpu.VMEM((PIECES, 2 * NFFT, 256), BF16),
            pltpu.VMEM((TAPS * Q, 128), F32),
            pltpu.VMEM((FRAMES * LOCAL * Q, 128), F32),
            pltpu.VMEM((FRAMES * LOCAL, 2 * NFFT), BF16),
            pltpu.VMEM((TM, SPILL_ROWS, 128), BF16),
            pltpu.VMEM((TM, SPILL_ROWS, 128), BF16),
            pltpu.VMEM((TM, OWN_ROWS, 128), BF16),
            pltpu.VMEM((TM, OWN_ROWS, 128), BF16),
            pltpu.VMEM((TILES, INPUTS, 128), BF16),
            pltpu.VMEM((2 * K, INPUTS), F32),
            pltpu.VMEM((TILES, INPUTS, 128), BF16),
            pltpu.VMEM((2, LOCAL, 128), BF16),
            pltpu.VMEM((LOCAL, 128), BF16),
            pltpu.VMEM((INPUTS, 128), BF16),
            pltpu.VMEM((2 * K, INPUTS), BF16),
            pltpu.VMEM((TM, 2 * K, INPUTS), BF16),
            pltpu.VMEM((TM, 8, 128), F32),
            pltpu.VMEM((TM, 8, 128), F32),
            dma((PARTS,)),
            dma((3,)),
            dma,
            dma,
            dma((TM,)),
            dma,
            dma((TM,)),
            dma((TILES,)),
            dma((TILES,)),
            dma((4,)),
            dma((2,)),
            dma,
            dma,
        ],
        compiler_params=pltpu.CompilerParams(
            collective_id=0, has_side_effects=True, vmem_limit_bytes=LIMIT * 1024 * 1024
        ),
        name="channelise",
    )(volt, taps, table, ref_chan, basis_in)


def write_kernel(cov_in, proj_in, power_in, cov, proj, power, sem):
    pieces = []
    for ch in range(2):
        for half in range(2):
            rows = pl.ds(half * (INPUTS // 2), INPUTS // 2)
            pieces.append(
                pltpu.make_async_copy(cov_in.at[ch, rows], cov.at[ch, rows], sem.at[ch * 2 + half])
            )
    for piece in pieces:
        piece.start()
    proj[...] = proj_in[...]
    power[...] = power_in[...]
    for piece in pieces:
        piece.wait()


def write(cov, proj, power):
    vmem = pl.BlockSpec(memory_space=pltpu.VMEM)
    whole = pl.BlockSpec(memory_space=pl.ANY)
    return pl.pallas_call(
        write_kernel,
        out_shape=tuple(jax.ShapeDtypeStruct(a.shape, a.dtype) for a in (cov, proj, power)),
        in_specs=[whole, vmem, vmem],
        out_specs=(whole, vmem, vmem),
        scratch_shapes=[pltpu.SemaphoreType.DMA((4,))],
        name="write",
    )(cov, proj, power)


FINAL = False


def on_device(table, voltages, filter_taps, reference_channel, basis_inputs):
    volt = voltages.reshape(LOCAL, 2, FRAMES * SUB, 128).transpose(0, 2, 1, 3).reshape(-1, 128)
    results = channelise(volt, filter_taps, table, reference_channel, basis_inputs)
    return write(*results) if FINAL else results


def solution(mesh):
    table = transform_table()

    def whole(voltages, filter_taps, reference_channel, basis_inputs):
        return jax.shard_map(
            on_device,
            mesh=mesh,
            in_specs=(P(), P("stn", None, "tm"), P(), P(), P()),
            out_specs=(P(("stn", "tm"), None, None), P(("stn", "tm"), None), P("stn", "tm")),
            check_vma=False,
        )(jnp.asarray(table), voltages, filter_taps, reference_channel, basis_inputs)

    return whole
```

time: 60.9 us -> 54.5 us (0.89)
  the two profiles are of different devices: /device:TPU:4 before, /device:TPU:1 now
where the time goes in v3:
time: 54.5 us; the launch traced here: 54.4 us
  Pallas kernels  48.9 us (90%)
  local copies, waits for them, and re-layouts  4.25 us (8%)
  between operations  1.3 us (2%)
    pallas_call x1, Pallas kernels, channelise(): pl.pallas_call(channelise_kernel, out_shape=(jax.ShapeDtypeStruct((2, INP...  48.9 us
    unnamed x7, local copies, waits for them, and re-layouts  4.25 us

profile of v3, /device:TPU:1, one launch (start us, length us, event | category | flops | bytes accessed | tf_op | source)
XLA Modules:
  0.0 54.4 jit_solution(15634490245453909616)
XLA Ops:
  1.3 48.9 %channelise.1 = (bf16[2,512,1024]{2,1,0:T(8,128)(2,1)}, f32[2,128]{1,0:T(2,128)}, f32[16,16]{1,0:T(8,128)}) custom-call(s32[4096,128]{1,0:T(8,128)} %bitcast.5, f32[16,1024]{1,0:T(8,128)} %taps_hbm.1, bf16[4,2048,256]{2,1,0:T(8,128)(2,1)} %constant.2.clone.table_hbm, s32[1]{0:T(128)S(6)} %copy.12.ref_hbm, s32[8]{0:T(128)} %basis_hbm.1), custom_call_target="tpu_custom_call" | custom-call | tf_op jit(solution)/shard_map/channelise/pallas_call | solution.py:457
  50.1 0.0 copy-start.1
  50.2 0.0 copy-start
  50.2 3.1 %copy.13 = bf16[2,512,1024]{2,1,0:T(8,128)(2,1)} copy(bf16[2,512,1024]{2,1,0:T(8,128)(2,1)} %get-tuple-element.6) | data formatting | bytes 4194304
  53.3 0.0 copy-done.1
  53.3 0.6 %copy.14 = f32[2,128]{1,0:T(2,128)} copy(f32[2,128]{1,0:T(2,128)S(1)} %copy-done.1) | data formatting | bytes 2048
  53.8 0.0 copy-done
  53.8 0.6 %copy.15 = f32[16,16]{1,0:T(8,128)} copy(f32[16,16]{1,0:T(8,128)S(1)} %copy-done) | data formatting | bytes 2048
Async XLA Ops:
  50.1 3.1 %copy-start.1 = (f32[2,128]{1,0:T(2,128)S(1)}, f32[2,128]{1,0:T(2,128)}, u32[]{:S(2)}) copy-start(f32[2,128]{1,0:T(2,128)} %get-tuple-element.7) | copy-start | bytes 3076
  50.2 3.7 %copy-start = (f32[16,16]{1,0:T(8,128)S(1)}, f32[16,16]{1,0:T(8,128)}, u32[]{:S(2)}) copy-start(f32[16,16]{1,0:T(8,128)} %get-tuple-element.8) | copy-start | bytes 3076

commit v4 on v3

--- a/solution.py
+++ b/solution.py
@@ -28,7 +28,7 @@
 PIECES = 4
 TILES = TM // 2
 OWN_ROWS, SPILL_ROWS = FRAMES * LOCAL, SPILL * LOCAL
-LIMIT = 60
+LIMIT = 56
 MESH = pl.DeviceIdType.MESH
 F32 = jnp.float32
 BF16 = jnp.bfloat16
@@ -79,7 +79,7 @@
     return vec_re, vec_im
 
 
-def covariances(v, basis, cov, proj):
+def covariances(v, basis, cov, proj, done):
     lane4 = lax.broadcasted_iota(jnp.int32, (1, 512), 1)
     x = jnp.concatenate([v[m].astype(F32) for m in range(TILES)], axis=1)
     real = (lane4 & 1) == 0
@@ -93,6 +93,7 @@
                 left, x_low, (((1,), (1,)), ((), ())), preferred_element_type=F32
             )
             cov[ch, :, part * INPUTS : (part + 1) * INPUTS] = (prod * (1.0 / SPECTRA)).astype(BF16)
+        done(ch)
 
     b = basis[...]
     b0 = b.astype(BF16)
@@ -428,7 +429,7 @@
     def _(d):
         power_copy(lax.rem(t + d, TM)).start()
 
-    covariances(v, basis, cov, proj)
+    covariances(v, basis, cov, proj, lambda ch: None)
 
     bytes_of(pow_in.at[pl.ds(0, TM - 1)], pow_rs)
     for owner in range(TM):
@@ -457,9 +458,9 @@
     return pl.pallas_call(
         channelise_kernel,
         out_shape=(
-            jax.ShapeDtypeStruct((2, INPUTS, 2 * INPUTS), BF16),
-            jax.ShapeDtypeStruct((2, 2 * K * K), F32),
-            jax.ShapeDtypeStruct((16, FRAMES), F32),
+            pltpu.VMEM((2, INPUTS, 2 * INPUTS), BF16),
+            pltpu.VMEM((2, 2 * K * K), F32),
+            pltpu.VMEM((16, FRAMES), F32),
         ),
         in_specs=[hbm] * 5,
         out_specs=(vmem, vmem, vmem),
@@ -508,41 +509,38 @@
 
 
 def write_kernel(cov_in, proj_in, power_in, cov, proj, power, sem):
-    pieces = []
-    for ch in range(2):
-        for half in range(2):
-            rows = pl.ds(half * (INPUTS // 2), INPUTS // 2)
-            pieces.append(
-                pltpu.make_async_copy(cov_in.at[ch, rows], cov.at[ch, rows], sem.at[ch * 2 + half])
-            )
-    for piece in pieces:
-        piece.start()
+    def store(p):
+        rows = pl.ds(p % 2 * (INPUTS // 2), INPUTS // 2)
+        return pltpu.make_async_copy(cov_in.at[p // 2, rows], cov.at[p // 2, rows], sem.at[p])
+
+    for p in range(4):
+        store(p).start()
     proj[...] = proj_in[...]
     power[...] = power_in[...]
-    for piece in pieces:
-        piece.wait()
+    for p in range(4):
+        store(p).wait()
 
 
 def write(cov, proj, power):
     vmem = pl.BlockSpec(memory_space=pltpu.VMEM)
-    whole = pl.BlockSpec(memory_space=pl.ANY)
+    hbm = pl.BlockSpec(memory_space=pltpu.HBM)
     return pl.pallas_call(
         write_kernel,
         out_shape=tuple(jax.ShapeDtypeStruct(a.shape, a.dtype) for a in (cov, proj, power)),
-        in_specs=[whole, vmem, vmem],
-        out_specs=(whole, vmem, vmem),
+        in_specs=[vmem, vmem, vmem],
+        out_specs=(hbm, vmem, vmem),
         scratch_shapes=[pltpu.SemaphoreType.DMA((4,))],
+        compiler_params=pltpu.CompilerParams(vmem_limit_bytes=16 * 1024 * 1024),
         name="write",
     )(cov, proj, power)
 
 
-FINAL = False
-
-
 def on_device(table, voltages, filter_taps, reference_channel, basis_inputs):
     volt = voltages.reshape(LOCAL, 2, FRAMES * SUB, 128).transpose(0, 2, 1, 3).reshape(-1, 128)
+    volt = pltpu.with_memory_space_constraint(volt, pltpu.HBM)
+    table = pltpu.with_memory_space_constraint(table, pltpu.HBM)
     results = channelise(volt, filter_taps, table, reference_channel, basis_inputs)
-    return write(*results) if FINAL else results
+    return write(*results)
 
 
 def solution(mesh):

time: 54.5 us -> 50.8 us (0.932)
  local copies, waits for them, and re-layouts: 4.25 us -> 0 us
    unnamed x7 -> x0, local copies, waits for them, and re-layouts: 4.25 us -> none
    pallas_call x1 -> x2, Pallas kernels: 48.9 us -> 49.4 us  [the longest x1 47.5 us: channelise(): pl.pallas_call(channelise_kernel, out_shape=(pltpu.VMEM((2, INPUTS, 2 * I...]
where the time goes in v4:
time: 50.8 us; the launch traced here: 50.7 us
  Pallas kernels  49.4 us (97%)
  between operations  1.28 us (3%)
    pallas_call x1, Pallas kernels, channelise(): pl.pallas_call(channelise_kernel, out_shape=(pltpu.VMEM((2, INPUTS, 2 * I...  47.5 us
    pallas_call x1, Pallas kernels, write(): pl.pallas_call(write_kernel, out_shape=tuple((jax.ShapeDtypeStruct(a.shap...  1.95 us

profile of v4, /device:TPU:1, one launch (start us, length us, event | category | flops | bytes accessed | tf_op | source)
XLA Modules:
  0.0 50.7 jit_solution(4298454517055689348)
XLA Ops:
  1.3 47.5 %channelise.1 = (bf16[2,512,1024]{2,1,0:T(8,128)(2,1)S(1)}, f32[2,128]{1,0:T(2,128)S(1)}, f32[16,16]{1,0:T(8,128)S(1)}) custom-call(s32[4096,128]{1,0:T(8,128)} %bitcast.5, f32[16,1024]{1,0:T(8,128)} %taps_hbm.1, bf16[4,2048,256]{2,1,0:T(8,128)(2,1)} %constant.2.clone.table_hbm, s32[1]{0:T(128)S(6)} %copy.9.ref_hbm, s32[8]{0:T(128)} %basis_hbm.1), custom_call_target="tpu_custom_call" | custom-call | tf_op jit(solution)/shard_map/channelise/pallas_call | solution.py:458
  48.7 1.9 %write.1 = (bf16[2,512,1024]{2,1,0:T(8,128)(2,1)}, f32[2,128]{1,0:T(2,128)}, f32[16,16]{1,0:T(8,128)}) custom-call(bf16[2,512,1024]{2,1,0:T(8,128)(2,1)S(1)} %get-tuple-element.6.cov_in, f32[2,128]{1,0:T(2,128)S(1)} %get-tuple-element.7.proj_in, f32[16,16]{1,0:T(8,128)S(1)} %get-tuple-element.8.power_in), custom_call_target="tpu_custom_call" | custom-call | tf_op jit(solution)/shard_map/write/pallas_call | solution.py:527

commit v5 on v4

--- a/solution.py
+++ b/solution.py
@@ -122,7 +122,7 @@
     volt_hbm, taps_hbm, table_hbm, ref_hbm, basis_hbm,
     cov, proj, power,
     volt, taps, ref_chan, basis_in, table, tap_rows, frames_f, lhs, spill_out, spill_in, own_out, own_in,
-    v, basis, send1, ref_halo, ref_out, ref_in, cols_out, cols_in, pow_out, pow_in,
+    v, basis, send1, ref_halo, ref_out, ref_near, ref_pack, ref_in, cols_out, cols_in, pow_out, pow_in,
     volt_sem, small_sem, table_sem, spill_ss, spill_rs, own_ss, own_rs, ss1, rs1, ref_sem, cols_sem, pow_ss, pow_rs,
 ):
     s = lax.axis_index("stn")
@@ -248,13 +248,26 @@
             device_id_type=MESH,
         )
 
-    def ref_copy(to):
+    y, z, core = s // 8, lax.rem(s // 2, 4), lax.rem(s, 2)
+
+    def near_copy(d):
+        to = lax.rem(y * 2 + core + d, 8)
         return pltpu.make_async_remote_copy(
             src_ref=ref_out,
-            dst_ref=ref_in.at[pl.ds(pl.multiple_of(s * LOCAL, LOCAL), LOCAL)],
+            dst_ref=ref_near.at[core * 4 + y],
             send_sem=ref_sem.at[2],
             recv_sem=ref_sem.at[3],
-            device_id={"stn": to},
+            device_id={"stn": to // 2 * 8 + z * 2 + lax.rem(to, 2)},
+            device_id_type=MESH,
+        )
+
+    def far_copy(d):
+        return pltpu.make_async_remote_copy(
+            src_ref=ref_pack,
+            dst_ref=ref_in.at[pl.ds(pl.multiple_of(z * 2 * LOCAL, 2 * LOCAL), 2 * LOCAL)],
+            send_sem=ref_sem.at[4],
+            recv_sem=ref_sem.at[5],
+            device_id={"stn": y * 8 + lax.rem(z + d, 4) * 2 + core},
             device_id_type=MESH,
         )
 
@@ -329,11 +342,26 @@
         bytes_of(ref_halo.at[1], ref_sem.at[1])
 
     ref_out[...] = (own_ref + ref_halo[1].astype(F32)).astype(BF16)
-    ref_in[pl.ds(pl.multiple_of(s * LOCAL, LOCAL), LOCAL), :] = ref_out[...]
-
-    @pl.loop(1, STN)
+    ref_near[core * 4 + y] = ref_out[...]
+
+    @pl.loop(1, 8)
     def _(d):
-        ref_copy(lax.rem(s + d, STN)).start()
+        near_copy(d).start()
+
+    def gather_far():
+        bytes_of(ref_near.at[pl.ds(0, 7)], ref_sem.at[3])
+        for c in range(2):
+            packed = jnp.zeros((LOCAL, 128), F32)
+            for group in range(4):
+                packed = packed + jnp.where(
+                    lane // 32 == group, ref_near[c * 4 + group].astype(F32), 0.0
+                )
+            ref_pack[c * LOCAL : (c + 1) * LOCAL, :] = packed.astype(BF16)
+        ref_in[pl.ds(pl.multiple_of(z * 2 * LOCAL, 2 * LOCAL), 2 * LOCAL), :] = ref_pack[...]
+
+        @pl.loop(1, 4)
+        def _(d):
+            far_copy(d).start()
 
     def turn(step):
         m = lax.rem(t // 2 + step, TILES)
@@ -363,21 +391,27 @@
             turn_copy(m, lax.rem(s + d, STN)).start()
 
     def send_columns():
-        bytes_of(ref_in.at[pl.ds(0, INPUTS - LOCAL)], ref_sem.at[3])
+        bytes_of(ref_in.at[pl.ds(0, 6 * LOCAL)], ref_sem.at[5])
         row16 = lax.broadcasted_iota(jnp.int32, (2 * K, 1), 0)
         wanted = jnp.zeros((2 * K, 1), jnp.int32)
         for k in range(K):
             wanted = jnp.where(lax.rem(row16, K) == k, basis_in[k], wanted)
-        column = lax.broadcasted_iota(jnp.int32, (2 * K, INPUTS), 1)
-        onehot = jnp.where(column == wanted, 1.0, 0.0).astype(BF16)
+        column = lax.broadcasted_iota(jnp.int32, (2 * K, 128), 1)
+        onehot = jnp.where(column == lax.rem(wanted, 128), 1.0, 0.0).astype(BF16)
         block = ref_in[...]
         picked = jnp.dot(onehot, block, preferred_element_type=F32)
+        picked = jnp.where(lane // 32 == wanted // 128, picked, 0.0)
+        picked = picked + pltpu.roll(picked, 64, 1)
+        picked = picked + pltpu.roll(picked, 32, 1)
         swapped = jnp.where((lane & 1) == 0, -pltpu.roll(picked, 127, 1), pltpu.roll(picked, 1, 1))
         left = jnp.where(row16 < K, picked, swapped)
-        left = jnp.where(lane < 2 * FRAMES, left, 0.0).astype(BF16)
-        columns = lax.dot_general(
-            left, block, (((1,), (1,)), ((), ())), preferred_element_type=F32
-        ).astype(BF16)
+        parts = []
+        for group in range(4):
+            own = jnp.where(lane // 32 == group, left, 0.0).astype(BF16)
+            parts.append(
+                lax.dot_general(own, block, (((1,), (1,)), ((), ())), preferred_element_type=F32)
+            )
+        columns = jnp.concatenate(parts, axis=1).astype(BF16)
         cols_out[...] = columns
         cols_in[t] = columns
 
@@ -395,6 +429,7 @@
         basis[0:K, :] = basis_re
         basis[K:, :] = basis_im
 
+    gather_far()
     for step in range(TILES):
         turn(step)
         if step == COLUMNS_AT:
@@ -436,7 +471,8 @@
         power[2 * owner : 2 * owner + 2, :] = pow_in[owner, 0:2, 0:FRAMES]
 
     bytes_of(cols_in.at[pl.ds(0, TM - 1)], cols_sem.at[0])
-    bytes_of(ref_in.at[pl.ds(0, INPUTS - LOCAL)], ref_sem.at[2])
+    bytes_of(ref_near.at[pl.ds(0, 7)], ref_sem.at[2])
+    bytes_of(ref_in.at[pl.ds(0, 6 * LOCAL)], ref_sem.at[4])
 
     bytes_of(pow_out.at[pl.ds(0, TM - 1)], pow_ss)
     bytes_of(own_out.at[pl.ds(0, TM - 1)], own_ss)
@@ -482,7 +518,9 @@
             pltpu.VMEM((TILES, INPUTS, 128), BF16),
             pltpu.VMEM((2, LOCAL, 128), BF16),
             pltpu.VMEM((LOCAL, 128), BF16),
-            pltpu.VMEM((INPUTS, 128), BF16),
+            pltpu.VMEM((8, LOCAL, 128), BF16),
+            pltpu.VMEM((2 * LOCAL, 128), BF16),
+            pltpu.VMEM((8 * LOCAL, 128), BF16),
             pltpu.VMEM((2 * K, INPUTS), BF16),
             pltpu.VMEM((TM, 2 * K, INPUTS), BF16),
             pltpu.VMEM((TM, 8, 128), F32),
@@ -496,7 +534,7 @@
             dma((TM,)),
             dma((TILES,)),
             dma((TILES,)),
-            dma((4,)),
+            dma((6,)),
             dma((2,)),
             dma,
             dma,

time: 50.8 us -> 49.6 us (0.976)
  Pallas kernels: 49.4 us -> 48.2 us
    pallas_call x1, Pallas kernels: 47.5 us -> 46.2 us  [channelise(): pl.pallas_call(channelise_kernel, out_shape=(pltpu.VMEM((2, INPUTS, 2 * I...]
where the time goes in v5:
time: 49.6 us; the launch traced here: 49.5 us
  Pallas kernels  48.2 us (97%)
  between operations  1.28 us (3%)
    pallas_call x1, Pallas kernels, channelise(): pl.pallas_call(channelise_kernel, out_shape=(pltpu.VMEM((2, INPUTS, 2 * I...  46.2 us
    pallas_call x1, Pallas kernels, write(): pl.pallas_call(write_kernel, out_shape=tuple((jax.ShapeDtypeStruct(a.shap...  1.95 us

profile of v5, /device:TPU:1, one launch (start us, length us, event | category | flops | bytes accessed | tf_op | source)
XLA Modules:
  0.0 49.5 jit_solution(4242320994462884328)
XLA Ops:
  1.3 46.2 %channelise.1 = (bf16[2,512,1024]{2,1,0:T(8,128)(2,1)S(1)}, f32[2,128]{1,0:T(2,128)S(1)}, f32[16,16]{1,0:T(8,128)S(1)}) custom-call(s32[4096,128]{1,0:T(8,128)} %bitcast.5, f32[16,1024]{1,0:T(8,128)} %taps_hbm.1, bf16[4,2048,256]{2,1,0:T(8,128)(2,1)} %constant.2.clone.table_hbm, s32[1]{0:T(128)S(6)} %copy.9.ref_hbm, s32[8]{0:T(128)} %basis_hbm.1), custom_call_target="tpu_custom_call" | custom-call | tf_op jit(solution)/shard_map/channelise/pallas_call | solution.py:494
  47.5 1.9 %write.1 = (bf16[2,512,1024]{2,1,0:T(8,128)(2,1)}, f32[2,128]{1,0:T(2,128)}, f32[16,16]{1,0:T(8,128)}) custom-call(bf16[2,512,1024]{2,1,0:T(8,128)(2,1)S(1)} %get-tuple-element.6.cov_in, f32[2,128]{1,0:T(2,128)S(1)} %get-tuple-element.7.proj_in, f32[16,16]{1,0:T(8,128)S(1)} %get-tuple-element.8.power_in), custom_call_target="tpu_custom_call" | custom-call | tf_op jit(solution)/shard_map/write/pallas_call | solution.py:565

commit v6 on v5

--- a/solution.py
+++ b/solution.py
@@ -295,26 +295,27 @@
         preferred_element_type=F32,
     ).astype(BF16)
     ref_halo[0] = ref_tile(SPILL, ref_table).astype(BF16)
-    for piece in range(PIECES):
+    spill_in[0] = jnp.zeros((SPILL_ROWS, 128), BF16)
+    pl.semaphore_wait(barrier, STN - 1 + TM - 1)
+
+    @pl.when(t < TM - 1)
+    def _():
+        ref_halo_copy().start()
+
+    for step in range(PIECES):
+        piece = lax.rem(t // 2 + 1 + step, PIECES)
         part = jnp.dot(lhs[0:SPILL_ROWS, :], table[piece], preferred_element_type=F32).astype(BF16)
-        spill_out[2 * piece] = part[:, 0:128]
-        spill_out[2 * piece + 1] = part[:, 128:]
+        for b in range(2):
+            to = 2 * piece + b
+            spill_out[to] = part[:, b * 128 : (b + 1) * 128]
+
+            @pl.when((t < TM - 1) & (to != t))
+            def _():
+                spill_copy(to).start()
 
     @pl.when(t < TM - 1)
     def _():
         spill_in[t + 1] = spill_out[t]
-
-    spill_in[0] = jnp.zeros((SPILL_ROWS, 128), BF16)
-
-    pl.semaphore_wait(barrier, STN - 1 + TM - 1)
-
-    @pl.when(t < TM - 1)
-    def _():
-        ref_halo_copy().start()
-
-        @pl.loop(1, TM)
-        def _(d):
-            spill_copy(lax.rem(t + d, TM)).start()
 
     filter_frames(False)
 
@@ -364,7 +365,7 @@
             far_copy(d).start()
 
     def turn(step):
-        m = lax.rem(t // 2 + step, TILES)
+        m = lax.rem(t // 2 + TILES - 1 - step, TILES)
         blocks = []
         for b in range(2):
             block = 2 * m + b
@@ -386,9 +387,12 @@
         mine = pl.ds(pl.multiple_of(s * LOCAL, LOCAL), LOCAL)
         v[m, mine, :] = send1[m, mine, :]
 
-        @pl.loop(1, STN)
-        def _(d):
-            turn_copy(m, lax.rem(s + d, STN)).start()
+        for away in (2, 1, 3, 0):
+            @pl.loop(0 if away else 1, 8)
+            def _(d):
+                near = lax.rem(y * 2 + core + d, 8)
+                to = near // 2 * 8 + lax.rem(z + away, 4) * 2 + lax.rem(near, 2)
+                turn_copy(m, to).start()
 
     def send_columns():
         bytes_of(ref_in.at[pl.ds(0, 6 * LOCAL)], ref_sem.at[5])
@@ -447,7 +451,7 @@
         0.0,
     )
     for step in range(TILES):
-        m = lax.rem(t // 2 + step, TILES)
+        m = lax.rem(t // 2 + TILES - 1 - step, TILES)
         bytes_of(v.at[m, pl.ds(0, INPUTS - LOCAL)], rs1.at[m])
         z = jnp.dot(low, v[m], preferred_element_type=F32)
         z_re = z[0:K] + pltpu.roll(z[K:], 127, 1)

time: 49.6 us -> 48.2 us (0.972)
  Pallas kernels: 48.2 us -> 46.8 us
    pallas_call x1, Pallas kernels: 46.2 us -> 44.8 us  [channelise(): pl.pallas_call(channelise_kernel, out_shape=(pltpu.VMEM((2, INPUTS, 2 * I...]
where the time goes in v6:
time: 48.2 us; the launch traced here: 48.1 us
  Pallas kernels  46.8 us (97%)
  between operations  1.28 us (3%)
    pallas_call x1, Pallas kernels, channelise(): pl.pallas_call(channelise_kernel, out_shape=(pltpu.VMEM((2, INPUTS, 2 * I...  44.8 us
    pallas_call x1, Pallas kernels, write(): pl.pallas_call(write_kernel, out_shape=tuple((jax.ShapeDtypeStruct(a.shap...  1.95 us

profile of v6, /device:TPU:1, one launch (start us, length us, event | category | flops | bytes accessed | tf_op | source)
XLA Modules:
  0.0 48.1 jit_solution(7720703814909258301)
XLA Ops:
  1.3 44.8 %channelise.1 = (bf16[2,512,1024]{2,1,0:T(8,128)(2,1)S(1)}, f32[2,128]{1,0:T(2,128)S(1)}, f32[16,16]{1,0:T(8,128)S(1)}) custom-call(s32[4096,128]{1,0:T(8,128)} %bitcast.5, f32[16,1024]{1,0:T(8,128)} %taps_hbm.1, bf16[4,2048,256]{2,1,0:T(8,128)(2,1)} %constant.2.clone.table_hbm, s32[1]{0:T(128)S(6)} %copy.9.ref_hbm, s32[8]{0:T(128)} %basis_hbm.1), custom_call_target="tpu_custom_call" | custom-call | tf_op jit(solution)/shard_map/channelise/pallas_call | solution.py:498
  46.1 1.9 %write.1 = (bf16[2,512,1024]{2,1,0:T(8,128)(2,1)}, f32[2,128]{1,0:T(2,128)}, f32[16,16]{1,0:T(8,128)}) custom-call(bf16[2,512,1024]{2,1,0:T(8,128)(2,1)S(1)} %get-tuple-element.6.cov_in, f32[2,128]{1,0:T(2,128)S(1)} %get-tuple-element.7.proj_in, f32[16,16]{1,0:T(8,128)S(1)} %get-tuple-element.8.power_in), custom_call_target="tpu_custom_call" | custom-call | tf_op jit(solution)/shard_map/write/pallas_call | solution.py:569

commit v7 on v6

--- a/solution.py
+++ b/solution.py
@@ -145,9 +145,12 @@
 
     barrier = pltpu.get_barrier_semaphore()
 
-    @pl.loop(1, STN)
-    def _(d):
-        pl.semaphore_signal(barrier, 1, device_id={"stn": lax.rem(s + d, STN)}, device_id_type=MESH)
+    for away in (2, 1, 3, 0):
+        @pl.loop(0 if away else 1, 8)
+        def _(d):
+            near = lax.rem(s // 8 * 2 + lax.rem(s, 2) + d, 8)
+            to = near // 2 * 8 + lax.rem(s // 2 + away, 4) * 2 + lax.rem(near, 2)
+            pl.semaphore_signal(barrier, 1, device_id={"stn": to}, device_id_type=MESH)
 
     @pl.loop(1, TM)
     def _(d):

time: 48.2 us -> 48.2 us (level)
  no operation moved by 1% of the time
where the time goes in v7:
time: 48.2 us; the launch traced here: 48.1 us
  Pallas kernels  46.8 us (97%)
  between operations  1.28 us (3%)
    pallas_call x1, Pallas kernels, channelise(): pl.pallas_call(channelise_kernel, out_shape=(pltpu.VMEM((2, INPUTS, 2 * I...  44.8 us
    pallas_call x1, Pallas kernels, write(): pl.pallas_call(write_kernel, out_shape=tuple((jax.ShapeDtypeStruct(a.shap...  1.95 us

profile of v7, /device:TPU:1, one launch (start us, length us, event | category | flops | bytes accessed | tf_op | source)
XLA Modules:
  0.0 48.1 jit_solution(14569597314783511681)
XLA Ops:
  1.3 44.8 %channelise.1 = (bf16[2,512,1024]{2,1,0:T(8,128)(2,1)S(1)}, f32[2,128]{1,0:T(2,128)S(1)}, f32[16,16]{1,0:T(8,128)S(1)}) custom-call(s32[4096,128]{1,0:T(8,128)} %bitcast.5, f32[16,1024]{1,0:T(8,128)} %taps_hbm.1, bf16[4,2048,256]{2,1,0:T(8,128)(2,1)} %constant.2.clone.table_hbm, s32[1]{0:T(128)S(6)} %copy.9.ref_hbm, s32[8]{0:T(128)} %basis_hbm.1), custom_call_target="tpu_custom_call" | custom-call | tf_op jit(solution)/shard_map/channelise/pallas_call | solution.py:501
  46.1 1.9 %write.1 = (bf16[2,512,1024]{2,1,0:T(8,128)(2,1)}, f32[2,128]{1,0:T(2,128)}, f32[16,16]{1,0:T(8,128)}) custom-call(bf16[2,512,1024]{2,1,0:T(8,128)(2,1)S(1)} %get-tuple-element.6.cov_in, f32[2,128]{1,0:T(2,128)S(1)} %get-tuple-element.7.proj_in, f32[16,16]{1,0:T(8,128)S(1)} %get-tuple-element.8.power_in), custom_call_target="tpu_custom_call" | custom-call | tf_op jit(solution)/shard_map/write/pallas_call | solution.py:572
